TPU v7x, 32 devices: a whole 2x2x4 slice. The times are simulated.
32 devices in a mesh: row: 8 (over y, x, core), col: 4 (over z).
Axes of the slice: x: 2, y: 2, z: 4, core: 2. Of those that a mesh axis runs over, the one named last changes fastest.
Arguments:
- gram_panel: float32 [2048, 1024], P('row', 'col'), may hold values from -1495.4 to 1495.4, as said below
- left_factor: bfloat16 [2048, 4096], P('row', 'col'), may hold values from -0.6 to 0.6
- solved_prev: bfloat16 [4096, 2048], P('row', 'col'), may hold values from -0.59765625 to 0.59765625
- right_block: float32 [1024, 2048], P('row', 'col'), may hold values from -6 to 6
Outputs:
- panel_factor: float32 [2048, 1024], P('row', 'col')
- solved_panel: float32 [1024, 2048], P('row', 'col')
Inputs may be any that keep to these rules, and one draw needn't show every extreme that they name: The rows of gram_panel at the panel's indices minus the product of the corresponding rows of left_factor with their transpose form a symmetric positive definite matrix.
All inputs are finite; a program needn't handle non-finite values.
Results may differ from a plain program's by a relative error of at most 0.0006.
Values may be sent and summed in bfloat16 or wider, within the bound.
A program may use at most 64 MiB of HBM per device.

v0:
```python
import jax
import jax.numpy as jnp
from jax import lax
from jax.sharding import PartitionSpec as P


def spread(value, axis, source):
    kept = jnp.where(lax.axis_index(axis) == source, value, 0).astype(value.dtype)
    return lax.psum(kept, axis)


def invert(diagonal):
    factor = jnp.linalg.cholesky(diagonal)
    identity = jnp.eye(diagonal.shape[0], dtype=jnp.float32)
    return jax.scipy.linalg.solve_triangular(factor, identity, lower=True)


def body(gram_panel, left_factor, solved_prev, right_block):
    row_count = lax.axis_size("row")
    col_count = lax.axis_size("col")
    row_place = lax.axis_index("row")
    col_place = lax.axis_index("col")
    block_rows = right_block.shape[0]
    col_width = gram_panel.shape[1]
    per_column = row_count // col_count
    strip_width = left_factor.shape[1] // per_column
    chosen = lax.all_gather(left_factor[:block_rows], "row", axis=0, tiled=True)
    portion = chosen
    summed = lax.psum_scatter(
        jnp.einsum("pk,mk->pm", portion, left_factor, preferred_element_type=jnp.float32),
        "col",
        scatter_dimension=0,
        tiled=True,
    )
    update = gram_panel - summed.T
    diag_part = lax.all_gather(update[:block_rows], "row", axis=0, tiled=True)
    diagonal = lax.all_gather(diag_part, "col", axis=1, tiled=True)
    inverse = invert(diagonal)
    inverse_cols = lax.dynamic_slice_in_dim(inverse, col_place * col_width, col_width, 0)
    inverse_part = inverse_cols
    panel_factor = lax.dot_general(
        lax.all_gather(update, "col", axis=1, tiled=True),
        inverse_part,
        (((1,), (1,)), ((), ())),
        precision=lax.Precision.HIGHEST,
    )
    strip_piece = lax.dynamic_slice_in_dim(
        chosen, row_place % per_column * strip_width, strip_width, 1
    )
    strip_piece = spread(strip_piece, "col", row_place // per_column)
    portion = strip_piece
    reduced = right_block - lax.psum_scatter(
        jnp.dot(portion, solved_prev, preferred_element_type=jnp.float32),
        "row",
        scatter_dimension=0,
        tiled=True,
    )
    inverse_rows = lax.dynamic_slice_in_dim(inverse, row_place * block_rows, block_rows, 0)
    inverse_part = inverse_rows
    solved_panel = jnp.dot(
        inverse_part,
        lax.all_gather(reduced, "row", axis=0, tiled=True),
        precision=lax.Precision.HIGHEST,
    )
    return (panel_factor, solved_panel)


def solution(mesh):
    in_specs = (P("row", "col"), P("row", "col"), P("row", "col"), P("row", "col"))
    out_specs = (P("row", "col"), P("row", "col"))
    return jax.shard_map(body, mesh=mesh, in_specs=in_specs, out_specs=out_specs, check_vma=False)
```

profile of v0, /device:TPU:0, one launch (start us, length us, event | category | flops | bytes accessed | tf_op | source)
XLA Modules:
  0.0 642.1 jit_solution(6030888469832809581)
XLA Ops:
  9.0 32.1 %all-gather.6.cloned.1.call-done = bf16[1024,1024]{1,0:T(8,128)(2,1)} async-done(((bf16[128,1024]{1,0:T(8,128)(2,1)}), bf16[1024,1024]{1,0:T(8,128)(2,1)}) %all-gather.6.cloned.1.call-update) | async-done | bytes 2097168 | tf_op jit(solution)/shard_map/all_gather | solution.py:27
  41.1 3.5 fusion.77
  46.2 25.7 %reduce-scatter.3.cloned.1.call-done = f32[256,256]{1,0:T(8,128)} async-done(((f32[1024,256]{1,0:T(8,128)}), f32[256,256]{1,0:T(8,128)}) %reduce-scatter.3.cloned.1.call-update) | async-done | bytes 262160 | tf_op jit(solution)/shard_map/reduce_scatter | solution.py:29
  73.8 51.2 %all-reduce.3.cloned.1.call-done = bf16[1024,512]{1,0:T(8,128)(2,1)} async-done(((bf16[1024,512]{1,0:T(8,128)(2,1)}), bf16[1024,512]{1,0:T(8,128)(2,1)}) %all-reduce.3.cloned.1.call-update) | async-done | bytes 1048592 | tf_op jit(solution)/shard_map/psum | solution.py:9
  125.0 3.3 fusion.78
  128.3 21.9 %all-gather.10.cloned.1.call-done = f32[1024,256]{0,1:T(8,128)} async-done(((f32[128,256]{0,1:T(8,128)}), f32[1024,256]{0,1:T(8,128)}) %all-gather.10.cloned.1.call-update) | async-done | bytes 1048592 | tf_op jit(solution)/shard_map/all_gather | solution.py:36
  150.3 44.3 %reduce-scatter.5.cloned.1.call-done = f32[128,512]{1,0:T(8,128)} async-done(((f32[1024,512]{1,0:T(8,128)}), f32[128,512]{1,0:T(8,128)}) %reduce-scatter.5.cloned.1.call-update) | async-done | bytes 262160 | tf_op jit(solution)/shard_map/reduce_scatter | solution.py:52
  196.8 2.4 fusion.21
  199.2 77.7 %all-gather.12.cloned.1.call-done = f32[1024,1024]{0,1:T(8,128)} async-done(((f32[1024,256]{0,1:T(8,128)}), f32[1024,1024]{0,1:T(8,128)}) %all-gather.12.cloned.1.call-update) | async-done | bytes 4194320 | tf_op jit(solution)/shard_map/all_gather | solution.py:37
  277.0 5.5 copy.7
  282.4 4.6 fusion
  289.0 11.7 %cholesky.223 = f32[128,128]{1,0:T(8,128)S(1)} custom-call(f32[128,128]{1,0:T(8,128)S(1)} %cholesky.580), custom_call_target="Cholesky" | custom-call | tf_op jit(solution)/shard_map/jit(cholesky)/cholesky | solution.py:13
  300.8 9.8 %custom-call.63 = f32[1,128,128]{1,2,0:T(8,128)S(1)} custom-call(f32[1,128,128]{2,1,0:T(8,128)S(1)} %get-tuple-element.66), custom_call_target="InvertDiagBlocksLowerTriangular" | custom-call | tf_op jit(solution)/shard_map/jit(cholesky)/cholesky | solution.py:13
  310.6 2.5 cholesky.255
  313.1 2.3 constant_dynamic-update-slice_fusion.28
  317.0 11.9 %cholesky.244 = f32[128,128]{1,0:T(8,128)S(1)} custom-call(f32[128,128]{1,0:T(8,128)S(1)} %cholesky.584), custom_call_target="Cholesky" | custom-call | tf_op jit(solution)/shard_map/jit(cholesky)/cholesky | solution.py:13
  329.6 9.8 %custom-call.64 = f32[1,128,128]{1,2,0:T(8,128)S(1)} custom-call(f32[1,128,128]{2,1,0:T(8,128)S(1)} %get-tuple-element.63), custom_call_target="InvertDiagBlocksLowerTriangular" | custom-call | tf_op jit(solution)/shard_map/jit(cholesky)/cholesky | solution.py:13
  342.7 11.7 %cholesky.468 = f32[128,128]{1,0:T(8,128)S(1)} custom-call(f32[128,128]{1,0:T(8,128)S(1)} %cholesky.589), custom_call_target="Cholesky" | custom-call | tf_op jit(solution)/shard_map/jit(cholesky)/cholesky | solution.py:13
  355.8 9.8 %custom-call.65 = f32[1,128,128]{1,2,0:T(8,128)S(1)} custom-call(f32[1,128,128]{2,1,0:T(8,128)S(1)} %get-tuple-element.60), custom_call_target="InvertDiagBlocksLowerTriangular" | custom-call | tf_op jit(solution)/shard_map/jit(cholesky)/cholesky | solution.py:13
  366.8 2.3 convolution_subtract_fusion.7
  369.2 12.1 %cholesky.487 = f32[128,128]{1,0:T(8,128)S(1)} custom-call(f32[128,128]{1,0:T(8,128)S(1)} %cholesky.594), custom_call_target="Cholesky" | custom-call | tf_op jit(solution)/shard_map/jit(cholesky)/cholesky | solution.py:13
  382.5 9.8 %custom-call.66 = f32[1,128,128]{1,2,0:T(8,128)S(1)} custom-call(f32[1,128,128]{2,1,0:T(8,128)S(1)} %get-tuple-element.57), custom_call_target="InvertDiagBlocksLowerTriangular" | custom-call | tf_op jit(solution)/shard_map/jit(cholesky)/cholesky | solution.py:13
  393.4 2.4 convolution_subtract_fusion.8
  395.8 11.7 %cholesky.506 = f32[128,128]{1,0:T(8,128)S(1)} custom-call(f32[128,128]{1,0:T(8,128)S(1)} %cholesky.599), custom_call_target="Cholesky" | custom-call | tf_op jit(solution)/shard_map/jit(cholesky)/cholesky | solution.py:13
  408.8 9.9 %custom-call.67 = f32[1,128,128]{1,2,0:T(8,128)S(1)} custom-call(f32[1,128,128]{2,1,0:T(8,128)S(1)} %get-tuple-element.54), custom_call_target="InvertDiagBlocksLowerTriangular" | custom-call | tf_op jit(solution)/shard_map/jit(cholesky)/cholesky | solution.py:13
  419.8 2.3 convolution_subtract_fusion.9
  422.0 11.7 %cholesky.526 = f32[128,128]{1,0:T(8,128)S(1)} custom-call(f32[128,128]{1,0:T(8,128)S(1)} %cholesky.604), custom_call_target="Cholesky" | custom-call | tf_op jit(solution)/shard_map/jit(cholesky)/cholesky | solution.py:13
  435.1 9.8 %custom-call.68 = f32[1,128,128]{1,2,0:T(8,128)S(1)} custom-call(f32[1,128,128]{2,1,0:T(8,128)S(1)} %get-tuple-element.51), custom_call_target="InvertDiagBlocksLowerTriangular" | custom-call | tf_op jit(solution)/shard_map/jit(cholesky)/cholesky | solution.py:13
  447.9 11.9 %cholesky.546 = f32[128,128]{1,0:T(8,128)S(1)} custom-call(f32[128,128]{1,0:T(8,128)S(1)} %cholesky.609), custom_call_target="Cholesky" | custom-call | tf_op jit(solution)/shard_map/jit(cholesky)/cholesky | solution.py:13
  461.2 9.8 %custom-call.69 = f32[1,128,128]{1,2,0:T(8,128)S(1)} custom-call(f32[1,128,128]{2,1,0:T(8,128)S(1)} %get-tuple-element.48), custom_call_target="InvertDiagBlocksLowerTriangular" | custom-call | tf_op jit(solution)/shard_map/jit(cholesky)/cholesky | solution.py:13
  473.6 11.7 %cholesky.564 = f32[128,128]{1,0:T(8,128)S(1)} custom-call(f32[128,128]{1,0:T(8,128)S(1)} %convolution_subtract_fusion.11), custom_call_target="Cholesky" | custom-call | tf_op jit(solution)/shard_map/jit(cholesky)/cholesky | solution.py:13
  492.4 4.8 select_select_fusion
  497.3 22.5 %while.1 = (s32[]{:T(128)}, f32[1024,1024]{1,0:T(8,128)}, s32[8,2]{0,1:T(2,128)S(1)}, f32[8,128,128]{2,1,0:T(8,128)S(1)}, s32[]{:T(128)}) while((s32[]{:T(128)}, f32[1024,1024]{1,0:T(8,128)}, s32[8,2]{0,1:T(2,128)S(1)}, f32[8,128,128]{2,1,0:T(8,128)S(1)}, s32[]{:T(128)}) %tuple.61), condition=%wide.while_cond, body=%wide.while_body.sunk | while | flops 2 | bytes 131181 | solution.py:15
  497.9 2.2 bitcast_dynamic-update-slice_fusion.2
  500.7 2.2 bitcast_dynamic-update-slice_fusion.2
  503.5 2.2 bitcast_dynamic-update-slice_fusion.2
  506.3 2.2 bitcast_dynamic-update-slice_fusion.2
  509.1 2.2 bitcast_dynamic-update-slice_fusion.2
  512.0 2.2 bitcast_dynamic-update-slice_fusion.2
  514.8 2.2 bitcast_dynamic-update-slice_fusion.2
  517.6 2.1 bitcast_dynamic-update-slice_fusion.2
  519.7 79.0 %custom-call.70 = f32[8,128,128]{1,2,0:T(8,128)S(1)} custom-call(f32[8,128,128]{2,1,0:T(8,128)S(1)} %get-tuple-element.9), custom_call_target="InvertDiagBlocksLowerTriangular" | custom-call | tf_op jit(solution)/shard_map/jit(_solve_triangular)/triangular_solve | solution.py:15
  610.2 2.2 fusion.18
  614.0 2.6 convolution_subtract_fusion.2
  618.1 2.8 convolution_subtract_fusion.1
  622.4 3.4 convolution_subtract_fusion.3
  627.2 3.8 fusion.32
  631.0 4.1 fusion.26
  (101 shorter events, 54.5 us)
Async XLA Ops:
  7.2 117.8 %copy-start = (bf16[512,512]{1,0:T(8,128)(2,1)S(1)}, bf16[512,512]{1,0:T(8,128)(2,1)}, u32[]{:S(2)}) copy-start(bf16[512,512]{1,0:T(8,128)(2,1)} %param.6) | copy-start | bytes 1572868
  7.2 33.9 %all-gather.6.cloned.1.call-start = ((), (), s32[]{:S(2)}) async-start(), calls=%async_computation.2 | async-start | bytes 2359296 | tf_op jit(solution)/shard_map/all_gather | solution.py:27
  9.0 37.1 %copy-start.6 = (f32[256,256]{1,0:T(8,128)S(1)}, f32[256,256]{1,0:T(8,128)}, u32[]{:S(2)}) copy-start(f32[256,256]{1,0:T(8,128)} %param.4) | copy-start | bytes 786436
  9.0 63.0 %reduce-scatter.3.cloned.1.call-start = ((), (), s32[]{:S(2)}) async-start(), calls=%async_computation.3 | async-start | bytes 1310720 | tf_op jit(solution)/shard_map/reduce_scatter | solution.py:29
  41.1 3.7 copy-start.4
  44.7 80.3 %all-reduce.3.cloned.1.call-start = ((), (), s32[]{:S(2)}) async-start(), calls=%async_computation.7 | async-start | bytes 2097152 | tf_op jit(solution)/shard_map/psum | solution.py:9
  46.0 148.6 %copy-start.5 = (f32[128,512]{1,0:T(8,128)S(1)}, f32[128,512]{1,0:T(8,128)}, u32[]{:S(2)}) copy-start(f32[128,512]{1,0:T(8,128)} %param.7) | copy-start | bytes 786436
  46.0 104.2 %all-gather.10.cloned.1.call-start = ((), (), s32[]{:S(2)}) async-start(), calls=%async_computation.5 | async-start | bytes 1179648 | tf_op jit(solution)/shard_map/all_gather | solution.py:36
  73.0 123.8 %copy-start.3 = (f32[256,256]{0,1:T(8,128)}, f32[256,256]{0,1:T(8,128)S(1)}, u32[]{:S(2)}) copy-start(f32[256,256]{0,1:T(8,128)S(1)} %bitcast_subtract_fusion) | copy-start | bytes 786436
  73.7 121.0 %reduce-scatter.5.cloned.1.call-start = ((), (), s32[]{:S(2)}) async-start(), calls=%async_computation.8 | async-start | bytes 2359296 | tf_op jit(solution)/shard_map/reduce_scatter | solution.py:52
  128.3 148.7 %all-gather.12.cloned.1.call-start = ((), (), s32[]{:S(2)}) async-start(), calls=%async_computation.6 | async-start | bytes 5242880 | tf_op jit(solution)/shard_map/all_gather | solution.py:37
  150.3 476.9 %all-gather.14.cloned.1.call-start = ((), (), s32[]{:S(2)}) async-start(), calls=%async_computation.9 | async-start | bytes 2359296 | tf_op jit(solution)/shard_map/all_gather | solution.py:62
  196.4 434.6 %all-gather.8.cloned.1.call-start = ((), (), s32[]{:S(2)}) async-start(), calls=%async_computation.4 | async-start | bytes 1310720 | tf_op jit(solution)/shard_map/all_gather | solution.py:42
  287.1 2.0 copy-start.2
  598.7 4.7 copy-start.1
Sparse Core Ops, SparseCore 0:
  10.5 30.5 all-gather.5
  44.8 27.1 reduce-scatter.2
  74.5 50.4 all-reduce.2
  127.3 22.9 all-gather.9
  153.4 41.2 reduce-scatter.4
  196.2 80.7 all-gather.11
  279.6 26.5 all-gather.13
  308.4 27.7 all-gather.7
where the time goes:
time: 646 us; the launch traced here: 642 us
  other arithmetic  268 us (41%)
  waiting for transfers between devices  253 us (39%)
  matrix products  66.2 us (10%)
  local copies, waits for them, and re-layouts  34.9 us (5%)
  between operations  19.8 us (3%)
    another operation x30, other arithmetic, invert(): factor = jnp.linalg.cholesky(diagonal)  173 us
    another operation x3, other arithmetic, invert(): return jax.scipy.linalg.solve_triangular(factor, identity, lower=True)  83.8 us
    all_gather x1, waiting for transfers between devices, body(): diagonal = lax.all_gather(diag_part, 'col', axis=1, tiled=True)  77.7 us
    psum x1, waiting for transfers between devices, spread(): return lax.psum(kept, axis)  51.2 us
    reduce_scatter x1, waiting for transfers between devices, body(): lax.psum_scatter(jnp.dot(portion, solved_prev, preferred_element_type=jnp...  44.3 us
    all_gather x1, waiting for transfers between devices, body(): chosen = lax.all_gather(left_factor[:block_rows], 'row', axis=0, tiled=True)  32.1 us
    another operation x15, matrix products, invert(): return jax.scipy.linalg.solve_triangular(factor, identity, lower=True)  28.4 us
    reduce_scatter x1, waiting for transfers between devices, body(): lax.psum_scatter(jnp.einsum('pk,mk->pm', portion, left_factor, preferred_...  25.7 us
  transfers between devices with their start and end apart: 8, of which 6 were waited for; matrix products, arithmetic and copies ran while one was open for 56% of the time, Pallas kernels for 0%

commit v1 on v0

--- a/solution.py
+++ b/solution.py
@@ -1,18 +1,113 @@
+import functools
+
 import jax
 import jax.numpy as jnp
 from jax import lax
+from jax.experimental import pallas as pl
+from jax.experimental.pallas import tpu as pltpu
 from jax.sharding import PartitionSpec as P
+
+STRIP = 8
+TILE = 128
+
+
+def halves(value):
+    high = value.astype(jnp.bfloat16)
+    low = (value - high.astype(jnp.float32)).astype(jnp.bfloat16)
+    return high, low
+
+
+def dot3(left, right, dims=((1,), (0,))):
+    lh, ll = halves(left)
+    rh, rl = halves(right)
+    a = jnp.concatenate([lh, lh, ll], axis=dims[0][0])
+    b = jnp.concatenate([rh, rl, rh], axis=dims[1][0])
+    return lax.dot_general(a, b, (dims, ((), ())), preferred_element_type=jnp.float32)
+
+
+def invert_tile(a):
+    lane = lax.broadcasted_iota(jnp.int32, (STRIP, TILE), 1)
+    sub = lax.broadcasted_iota(jnp.int32, (STRIP, TILE), 0)
+    lane_all = lax.broadcasted_iota(jnp.int32, (TILE, TILE), 1)
+    done = []
+    for g in range(TILE // STRIP):
+        lo = g * STRIP
+        strip = a[:STRIP]
+        cols = [
+            jnp.broadcast_to(strip[:, lo + k : lo + k + 1], (STRIP, TILE)) for k in range(STRIP)
+        ]
+        t = jnp.where((lane >= lo) & (lane < lo + STRIP), (lane - lo == sub).astype(jnp.float32), strip)
+        out = jnp.zeros_like(t)
+        for j in range(STRIP):
+            pivot = jnp.broadcast_to(cols[j][j : j + 1], (STRIP, TILE))
+            inv = 1.0 / pivot
+            row = jnp.broadcast_to(t[j : j + 1], (STRIP, TILE))
+            out = jnp.where(sub == j, row * lax.rsqrt(pivot), out)
+            mult = jnp.where(sub == j, 1.0 - inv, cols[j] * inv)
+            t = t - mult * row
+            for k in range(j + 1, STRIP):
+                cols[k] = cols[k] - mult * jnp.broadcast_to(cols[k][j : j + 1], (STRIP, TILE))
+        done.append(jnp.where(lane < lo + STRIP, out, 0.0))
+        if lo + STRIP < TILE:
+            below = a[STRIP:]
+            rows = TILE - lo - STRIP
+            inside = (lane_all[:rows] >= lo) & (lane_all[:rows] < lo + STRIP)
+            sent = strip.T[lo + STRIP :]
+            a = jnp.where(inside, 0.0, below) - dot3(sent, t)
+    return jnp.concatenate(done, axis=0)
+
+
+def inverse_kernel(d_ref, o_ref, w_ref):
+    size = d_ref.shape[0]
+    count = size // TILE
+    w_ref[...] = d_ref[...]
+    lane = lax.broadcasted_iota(jnp.int32, (TILE, size), 1)
+    eye = (
+        lax.broadcasted_iota(jnp.int32, (TILE, TILE), 0)
+        == lax.broadcasted_iota(jnp.int32, (TILE, TILE), 1)
+    ).astype(jnp.float32)
+
+    def step(k, carry):
+        at = pl.multiple_of(k * TILE, TILE)
+        here = pl.ds(at, TILE)
+        small = invert_tile(w_ref[here, here])
+        w_ref[here, here] = eye
+        z = dot3(small, w_ref[here, :])
+        o_ref[here, :] = jnp.where(lane < at + TILE, z, 0.0)
+        w_ref[here, :] = z
+        zh, zl = halves(z)
+        right = jnp.concatenate([zh, zl, zh], axis=0)
+
+        def trail(i, c):
+            mine = pl.ds(pl.multiple_of(i * TILE, TILE), TILE)
+            yh, yl = halves(w_ref[here, mine].T)
+            left = jnp.concatenate([yh, yh, yl], axis=1)
+            w_ref[mine, here] = jnp.zeros((TILE, TILE), jnp.float32)
+            w_ref[mine, :] -= jnp.dot(left, right, preferred_element_type=jnp.float32)
+            return c
+
+        lax.fori_loop(k + 1, count, trail, 0)
+        return carry
+
+    lax.fori_loop(0, count, step, 0)
+
+
+def invert(diagonal):
+    size = diagonal.shape[0]
+    return pl.pallas_call(
+        inverse_kernel,
+        out_shape=jax.ShapeDtypeStruct((size, size), jnp.float32),
+        in_specs=[pl.BlockSpec(memory_space=pltpu.VMEM)],
+        out_specs=pl.BlockSpec(memory_space=pltpu.VMEM),
+        scratch_shapes=[pltpu.VMEM((size, size), jnp.float32)],
+        compiler_params=pltpu.CompilerParams(vmem_limit_bytes=40 * 1024 * 1024),
+        cost_estimate=pl.CostEstimate(flops=4 * size**3, bytes_accessed=8 * size * size, transcendentals=0),
+    )(diagonal)
 
 
 def spread(value, axis, source):
     kept = jnp.where(lax.axis_index(axis) == source, value, 0).astype(value.dtype)
     return lax.psum(kept, axis)
-
-
-def invert(diagonal):
-    factor = jnp.linalg.cholesky(diagonal)
-    identity = jnp.eye(diagonal.shape[0], dtype=jnp.float32)
-    return jax.scipy.linalg.solve_triangular(factor, identity, lower=True)
 
 
 def body(gram_panel, left_factor, solved_prev, right_block):

time: 646 us -> 349 us (0.54)
  other arithmetic: 268 us -> 3.92 us
  Pallas kernels: 0 us -> 53.3 us
  matrix products: 66.2 us -> 13.9 us
  local copies, waits for them, and re-layouts: 34.9 us -> 6.69 us
    another operation x33 -> x0, other arithmetic: 256 us -> none  [the longest x30 173 us: invert(): factor = jnp.linalg.cholesky(diagonal)]
    pallas_call x0 -> x1, Pallas kernels: none -> 53.3 us  [invert(): pl.pallas_call(inverse_kernel, out_shape=jax.ShapeDtypeStruct((size, size...]
    another operation x29 -> x0, matrix products: 51.5 us -> none  [the longest x15 28.4 us: invert(): return jax.scipy.linalg.solve_triangular(factor, identity, lower=True)]
    another operation x33 -> x0, local copies, waits for them, and re-layouts: 24.9 us -> none
  transfers between devices with their start and end apart: 8 -> 8, of which waited for: 6 -> 6; matrix products, arithmetic and copies ran while one was open for 56% -> 3% of each run, Pallas kernels for 0% -> 15%
where the time goes in v1:
time: 349 us; the launch traced here: 348 us
  waiting for transfers between devices  256 us (73%)
  Pallas kernels  53.3 us (15%)
  between operations  14.2 us (4%)
  matrix products  13.9 us (4%)
  local copies, waits for them, and re-layouts  6.69 us (2%)
  other arithmetic  3.92 us (1%)
    all_gather x1, waiting for transfers between devices, body(): diagonal = lax.all_gather(diag_part, 'col', axis=1, tiled=True)  80.6 us
    pallas_call x1, Pallas kernels, invert(): pl.pallas_call(inverse_kernel, out_shape=jax.ShapeDtypeStruct((size, size...  53.3 us
    psum x1, waiting for transfers between devices, spread(): return lax.psum(kept, axis)  51.2 us
    reduce_scatter x1, waiting for transfers between devices, body(): lax.psum_scatter(jnp.dot(portion, solved_prev, preferred_element_type=jnp...  43.5 us
    all_gather x1, waiting for transfers between devices, body(): chosen = lax.all_gather(left_factor[:block_rows], 'row', axis=0, tiled=True)  32.1 us
    reduce_scatter x1, waiting for transfers between devices, body(): lax.psum_scatter(jnp.einsum('pk,mk->pm', portion, left_factor, preferred_...  25.9 us
    all_gather x1, waiting for transfers between devices, body(): diag_part = lax.all_gather(update[:block_rows], 'row', axis=0, tiled=True)  21.8 us
  transfers between devices with their start and end apart: 8, of which 6 were waited for; matrix products, arithmetic and copies ran while one was open for 3% of the time, Pallas kernels for 15%

profile of v1, /device:TPU:0, one launch (start us, length us, event | category | flops | bytes accessed | tf_op | source)
XLA Modules:
  0.0 348.3 jit_solution(13537626045235355829)
XLA Ops:
  7.2 0.0 copy-start
  7.2 0.0 all-gather.6.cloned.1.call-start
  7.2 1.7 slice.6
  8.9 0.0 all-gather.6.cloned.1.call-update
  9.0 0.0 reduce-scatter.3.cloned.1.call-start
  9.0 32.1 %all-gather.6.cloned.1.call-done = bf16[1024,1024]{1,0:T(8,128)(2,1)} async-done(((bf16[128,1024]{1,0:T(8,128)(2,1)}), bf16[1024,1024]{1,0:T(8,128)(2,1)}) %all-gather.6.cloned.1.call-update) | async-done | bytes 2097168 | tf_op jit(solution)/shard_map/all_gather | solution.py:122
  41.1 0.0 copy-start.3
  41.1 3.6 %fusion.6 = f32[1024,256]{0,1:T(8,128)} fusion(bf16[1024,1024]{1,0:T(8,128)(2,1)} %all-gather.6.cloned.1.call-done, bf16[256,1024]{1,0:T(8,128)(2,1)} %param.5), kind=kOutput, calls=%fused_computation.8 | convolution fusion | flops 536870912 | bytes 3670016 | tf_op jit(solution)/shard_map/pk,mk->pm/dot_general | solution.py:125
  44.7 0.0 copy-start.5
  44.7 0.0 reduce-scatter.3.cloned.1.call-update
  44.7 0.0 all-reduce.2.cloned.1.call-start
  44.8 0.0 copy-done.3
  44.8 1.2 dynamic-slice_select_fusion
  46.0 0.0 all-reduce.2.cloned.1.call-update
  46.0 0.0 all-gather.10.cloned.1.call-start
  46.1 25.9 %reduce-scatter.3.cloned.1.call-done = f32[256,256]{0,1:T(8,128)} async-done(((f32[1024,256]{0,1:T(8,128)}), f32[256,256]{0,1:T(8,128)}) %reduce-scatter.3.cloned.1.call-update) | async-done | bytes 262160 | tf_op jit(solution)/shard_map/reduce_scatter | solution.py:124
  72.0 0.0 copy-done.5
  72.0 1.0 bitcast_subtract_fusion
  73.0 0.0 copy-start.4
  73.0 0.7 slice.8
  73.7 0.0 all-gather.10.cloned.1.call-update
  73.8 0.0 reduce-scatter.5.cloned.1.call-start
  73.8 51.2 %all-reduce.2.cloned.1.call-done = bf16[1024,512]{1,0:T(8,128)(2,1)} async-done(((bf16[1024,512]{1,0:T(8,128)(2,1)}), bf16[1024,512]{1,0:T(8,128)(2,1)}) %all-reduce.2.cloned.1.call-update) | async-done | bytes 1048592 | tf_op jit(solution)/shard_map/psum | solution.py:110
  125.0 0.0 copy-done
  125.0 3.3 fusion.7
  128.3 0.0 copy-start.6
  128.3 0.0 reduce-scatter.5.cloned.1.call-update
  128.3 0.0 copy-done.4
  128.3 0.0 all-gather.12.cloned.1.call-start
  128.4 21.8 %all-gather.10.cloned.1.call-done = f32[1024,256]{1,0:T(8,128)} async-done(((f32[128,256]{1,0:T(8,128)}), f32[1024,256]{1,0:T(8,128)}) %all-gather.10.cloned.1.call-update) | async-done | bytes 1048592 | tf_op jit(solution)/shard_map/all_gather | solution.py:131
  150.2 0.0 all-gather.12.cloned.1.call-update
  150.2 0.0 all-gather.8.cloned.1.call-start
  150.3 0.7 all-gather.8.cloned.1.call-update
  151.0 0.0 all-gather.14.cloned.1.call-start
  151.0 43.5 %reduce-scatter.5.cloned.1.call-done = f32[128,512]{1,0:T(8,128)} async-done(((f32[1024,512]{1,0:T(8,128)}), f32[128,512]{1,0:T(8,128)}) %reduce-scatter.5.cloned.1.call-update) | async-done | bytes 262160 | tf_op jit(solution)/shard_map/reduce_scatter | solution.py:147
  194.6 0.0 copy-done.6
  194.6 1.7 sub.12
  196.3 0.0 all-gather.14.cloned.1.call-update
  196.3 80.6 %all-gather.12.cloned.1.call-done.d_ref = f32[1024,1024]{1,0:T(8,128)} async-done(((f32[1024,256]{1,0:T(8,128)}), f32[1024,1024]{1,0:T(8,128)}) %all-gather.12.cloned.1.call-update) | async-done | bytes 4194320 | tf_op jit(solution)/shard_map/all_gather | solution.py:132
  276.9 0.0 copy-start.2
  276.9 2.2 copy-done.2
  279.1 53.3 %shard_map.59 = f32[1024,1024]{1,0:T(8,128)S(1)} custom-call(f32[1024,1024]{1,0:T(8,128)S(1)} %copy-done.2), custom_call_target="tpu_custom_call" | custom-call | flops 4294967296 | bytes 8388608 | tf_op jit(solution)/shard_map/pallas_call | solution.py:97
  332.4 0.0 copy-start.1
  332.4 2.0 copy-done.1
  334.4 0.0 all-gather.8.cloned.1.call-done
  334.4 3.3 fusion
  337.7 0.0 all-gather.14.cloned.1.call-done
  337.7 3.8 %fusion.2 = f32[128,512]{1,0:T(8,128)} fusion(f32[1024,512]{1,0:T(8,128)} %all-gather.14.cloned.1.call-done, f32[1024,1024]{1,0:T(8,128)} %copy-done.1, s32[]{:T(128)S(6)} %select_n.29), kind=kOutput, calls=%fused_computation.3 | convolution fusion | flops 805306368 | bytes 2883588 | tf_op jit(solution)/shard_map/dot_general | solution.py:155
Async XLA Ops:
  7.2 117.8 %copy-start = (bf16[512,512]{1,0:T(8,128)(2,1)S(1)}, bf16[512,512]{1,0:T(8,128)(2,1)}, u32[]{:S(2)}) copy-start(bf16[512,512]{1,0:T(8,128)(2,1)} %param.6) | copy-start | bytes 1572868
  7.2 33.9 %all-gather.6.cloned.1.call-start = ((), (), s32[]{:S(2)}) async-start(), calls=%async_computation.2 | async-start | bytes 2359296 | tf_op jit(solution)/shard_map/all_gather | solution.py:122
  9.0 63.0 %reduce-scatter.3.cloned.1.call-start = ((), (), s32[]{:S(2)}) async-start(), calls=%async_computation.3 | async-start | bytes 1310720 | tf_op jit(solution)/shard_map/reduce_scatter | solution.py:124
  41.1 3.7 %copy-start.3 = (bf16[1024,1024]{1,0:T(8,128)(2,1)S(1)}, bf16[1024,1024]{1,0:T(8,128)(2,1)}, u32[]{:S(2)}) copy-start(bf16[1024,1024]{1,0:T(8,128)(2,1)} %all-gather.6.cloned.1.call-done) | copy-start | bytes 6291460
  44.7 27.3 %copy-start.5 = (f32[256,256]{1,0:T(8,128)S(1)}, f32[256,256]{1,0:T(8,128)}, u32[]{:S(2)}) copy-start(f32[256,256]{1,0:T(8,128)} %param.4) | copy-start | bytes 786436
  44.7 80.3 %all-reduce.2.cloned.1.call-start = ((), (), s32[]{:S(2)}) async-start(), calls=%async_computation.7 | async-start | bytes 2097152 | tf_op jit(solution)/shard_map/psum | solution.py:110
  46.0 104.2 %all-gather.10.cloned.1.call-start = ((), (), s32[]{:S(2)}) async-start(), calls=%async_computation.5 | async-start | bytes 1179648 | tf_op jit(solution)/shard_map/all_gather | solution.py:131
  73.0 55.3 %copy-start.4 = (f32[256,256]{1,0:T(8,128)}, f32[256,256]{1,0:T(8,128)S(1)}, u32[]{:S(2)}) copy-start(f32[256,256]{1,0:T(8,128)S(1)} %bitcast_subtract_fusion) | copy-start | bytes 786436
  73.8 120.8 %reduce-scatter.5.cloned.1.call-start = ((), (), s32[]{:S(2)}) async-start(), calls=%async_computation.8 | async-start | bytes 2359296 | tf_op jit(solution)/shard_map/reduce_scatter | solution.py:147
  128.3 66.3 %copy-start.6 = (f32[128,512]{1,0:T(8,128)S(1)}, f32[128,512]{1,0:T(8,128)}, u32[]{:S(2)}) copy-start(f32[128,512]{1,0:T(8,128)} %param.7) | copy-start | bytes 786436
  128.3 148.6 %all-gather.12.cloned.1.call-start = ((), (), s32[]{:S(2)}) async-start(), calls=%async_computation.6 | async-start | bytes 5242880 | tf_op jit(solution)/shard_map/all_gather | solution.py:132
  150.2 184.2 %all-gather.8.cloned.1.call-start = ((), (), s32[]{:S(2)}) async-start(), calls=%async_computation.4 | async-start | bytes 1310720 | tf_op jit(solution)/shard_map/all_gather | solution.py:137
  151.0 186.7 %all-gather.14.cloned.1.call-start = ((), (), s32[]{:S(2)}) async-start(), calls=%async_computation.9 | async-start | bytes 2359296 | tf_op jit(solution)/shard_map/all_gather | solution.py:157
  276.9 2.2 copy-start.2
  332.4 2.0 copy-start.1
Sparse Core Ops, SparseCore 0:
  10.5 30.5 all-gather.5
  44.8 27.1 reduce-scatter.2
  74.5 50.4 all-reduce.1
  127.3 22.8 all-gather.9
  153.3 41.1 reduce-scatter.4
  196.1 80.7 all-gather.11
  279.1 26.5 all-gather.7
  307.8 27.7 all-gather.13

commit v2 on v1

--- a/solution.py
+++ b/solution.py
@@ -105,57 +105,223 @@
     )(diagonal)
 
 
-def spread(value, axis, source):
-    kept = jnp.where(lax.axis_index(axis) == source, value, 0).astype(value.dtype)
-    return lax.psum(kept, axis)
+MESH = pl.DeviceIdType.MESH
+
+
+def update_kernel(
+    rows_n, cols_n, left_ref, gram_ref, d_ref, low_ref, chosen, top_out, top_in, low_out, low_in,
+    top_all, low_all, c_send, c_recv, cs_send, cs_recv, t_send, t_recv, l_send, l_recv,
+    z_send, z_recv, y_send, y_recv, d_send, d_recv, ds_send, ds_recv,
+):
+    b, w = top_all.shape[1], top_all.shape[2]
+    pair = rows_n // cols_n
+    chips = rows_n // pair
+    r = lax.axis_index("row")
+    c = lax.axis_index("col")
+    core = r % pair
+    p = r // pair
+    sibling = p * pair + (pair - 1 - core)
+
+    def peer(s):
+        return ((p + s) % chips) * pair + core
+
+    def origin(s):
+        return (p + chips - s) % chips
+
+    barrier = pltpu.get_barrier_semaphore()
+    for s in range(1, chips):
+        pl.semaphore_signal(barrier, inc=1, device_id=(peer(s), c), device_id_type=MESH)
+    for u in range(1, cols_n):
+        pl.semaphore_signal(barrier, inc=1, device_id=(r, (c + u) % cols_n), device_id_type=MESH)
+    pl.semaphore_signal(barrier, inc=1, device_id=(sibling, c), device_id_type=MESH)
+    pl.semaphore_wait(barrier, chips + cols_n - 1)
+
+    def rows_of(ref, q):
+        return ref.at[pl.ds(pl.multiple_of(q * b, b), b)]
+
+    def copy(src, dst, send, recv, to):
+        return pltpu.make_async_remote_copy(
+            src_ref=src, dst_ref=dst, send_sem=send, recv_sem=recv, device_id=to, device_id_type=MESH
+        )
+
+    class Gather:
+        def __init__(self, ref, own, send, recv, side_send, side_recv):
+            self.ref, self.own = ref, own
+            self.sems = (send, recv, side_send, side_recv)
+
+        def far(self, s):
+            send, recv = self.sems[:2]
+            return copy(self.own, rows_of(self.ref, r), send.at[s], recv.at[s], (peer(s), c))
+
+        def far_in(self, s):
+            send, recv = self.sems[:2]
+            block = rows_of(self.ref, origin(s) * pair + core)
+            return copy(block, block, send.at[s], recv.at[s], (peer(s), c))
+
+        def near(self, s):
+            send, recv = self.sems[2:]
+            block = rows_of(self.ref, origin(s) * pair + core)
+            src = self.own if s == 0 else block
+            return copy(src, block, send.at[s], recv.at[s], (sibling, c))
+
+        def near_in(self, s):
+            send, recv = self.sems[2:]
+            block = rows_of(self.ref, origin(s) * pair + (pair - 1 - core))
+            return copy(block, block, send.at[s], recv.at[s], (sibling, c))
+
+        def start(self):
+            for s in range(1, chips):
+                self.far(s).start()
+            self.near(0).start()
+
+        def relay(self, s):
+            if s > 0:
+                self.far_in(s).wait_recv()
+                self.near(s).start()
+
+        def finish(self):
+            for s in range(chips):
+                if s > 0:
+                    self.far(s).wait_send()
+                self.near(s).wait_send()
+
+    def to_owner(q, out, into, send, recv):
+        return copy(out.at[q], into.at[c], send.at[q], recv.at[c], (r, q))
+
+    def from_owner(q, out, into, send, recv):
+        return copy(out.at[q], into.at[q], send.at[q], recv.at[q], (r, q))
+
+    def product(rows, q):
+        block = chosen[pl.ds(pl.multiple_of(q * w, w), w), :]
+        return lax.dot_general(
+            rows, block, (((1,), (1,)), ((), ())), preferred_element_type=jnp.float32
+        )
+
+    def total(start, out, into, sems):
+        value = start - out[c]
+        for u in range(1, cols_n):
+            q = (c + u) % cols_n
+            from_owner(q, out, into, *sems).wait_recv()
+            value = value - into[q]
+        return value
+
+    def share(ref, send, recv, u):
+        return copy(ref.at[c], ref.at[c], send.at[u], recv.at[u], (r, (c + u) % cols_n))
+
+    def shared(ref, send, recv, u):
+        block = ref.at[(c + cols_n - u) % cols_n]
+        return copy(block, block, send.at[u], recv.at[u], (r, (c + u) % cols_n))
+
+    top_sems, low_sems = (t_send, t_recv), (l_send, l_recv)
+    gather = Gather(chosen, left_ref.at[pl.ds(0, b)], c_send, c_recv, cs_send, cs_recv)
+    gather.start()
+    rows_of(chosen, r)[...] = left_ref[:b]
+    for s in range(chips):
+        gather.relay(s)
+        if s == 0:
+            gather.near_in(0).wait_recv()
+        for v in ((s,) if s < 1 else (s - 1,) if s > 1 else ()):
+            if v > 0:
+                gather.near_in(v).wait_recv()
+            top_out[origin(v)] = product(left_ref[:b], origin(v))
+
+            @pl.when(origin(v) != c)
+            def _(v=v):
+                to_owner(origin(v), top_out, top_in, *top_sems).start()
+
+    if chips > 1:
+        v = chips - 1
+        gather.near_in(v).wait_recv()
+        top_out[origin(v)] = product(left_ref[:b], origin(v))
+
+        @pl.when(origin(v) != c)
+        def _():
+            to_owner(origin(v), top_out, top_in, *top_sems).start()
+
+    for s in range(chips):
+        low_out[origin(s)] = product(left_ref[b:], origin(s))
+    top_all[c] = total(gram_ref[:b], top_out, top_in, top_sems)
+    for u in range(1, cols_n):
+        share(top_all, z_send, z_recv, u).start()
+    for u in range(1, cols_n):
+        q = (c + u) % cols_n
+        to_owner(q, low_out, low_in, *low_sems).start()
+    for u in range(1, cols_n):
+        shared(top_all, z_send, z_recv, u).wait_recv()
+    for q in range(cols_n):
+        d_ref[pl.ds(pl.multiple_of(r * b, b), b), q * w : (q + 1) * w] = top_all[q]
+    strips = Gather(d_ref, rows_of(d_ref, r), d_send, d_recv, ds_send, ds_recv)
+    strips.start()
+    low_all[c] = total(gram_ref[b:], low_out, low_in, low_sems)
+    for u in range(1, cols_n):
+        share(low_all, y_send, y_recv, u).start()
+    for s in range(chips):
+        strips.relay(s)
+    for u in range(1, cols_n):
+        shared(low_all, y_send, y_recv, u).wait_recv()
+    for q in range(cols_n):
+        low_ref[:, q * w : (q + 1) * w] = low_all[q]
+    for s in range(chips):
+        strips.near_in(s).wait_recv()
+    strips.finish()
+    gather.finish()
+    for u in range(1, cols_n):
+        q = (c + u) % cols_n
+        to_owner(q, top_out, top_in, *top_sems).wait_send()
+        to_owner(q, low_out, low_in, *low_sems).wait_send()
+        share(top_all, z_send, z_recv, u).wait_send()
+        share(low_all, y_send, y_recv, u).wait_send()
+
+
+def updated(left_factor, gram_panel, b):
+    rows_n, cols_n = lax.axis_size("row"), lax.axis_size("col")
+    rows, w = gram_panel.shape
+    size = rows_n * b
+    f32 = jnp.float32
+    vmem = pl.BlockSpec(memory_space=pltpu.VMEM)
+    chips = pltpu.SemaphoreType.DMA((cols_n,))
+    return pl.pallas_call(
+        functools.partial(update_kernel, rows_n, cols_n),
+        out_shape=(
+            jax.ShapeDtypeStruct((size, size), f32),
+            jax.ShapeDtypeStruct((rows - b, size), f32),
+        ),
+        in_specs=[vmem, vmem],
+        out_specs=(vmem, vmem),
+        scratch_shapes=[pltpu.VMEM((size, left_factor.shape[1]), jnp.bfloat16)]
+        + [pltpu.VMEM((cols_n, b, w), f32)] * 2
+        + [pltpu.VMEM((cols_n, rows - b, w), f32)] * 2
+        + [pltpu.VMEM((cols_n, b, w), f32), pltpu.VMEM((cols_n, rows - b, w), f32)]
+        + [chips] * 16,
+        compiler_params=pltpu.CompilerParams(
+            collective_id=0, has_side_effects=True, vmem_limit_bytes=48 * 1024 * 1024
+        ),
+        cost_estimate=pl.CostEstimate(flops=2 * size * rows * 1024, bytes_accessed=8 * 1024 * 1024, transcendentals=0),
+    )(left_factor, gram_panel)
 
 
 def body(gram_panel, left_factor, solved_prev, right_block):
-    row_count = lax.axis_size("row")
-    col_count = lax.axis_size("col")
     row_place = lax.axis_index("row")
     col_place = lax.axis_index("col")
-    block_rows = right_block.shape[0]
-    col_width = gram_panel.shape[1]
-    per_column = row_count // col_count
-    strip_width = left_factor.shape[1] // per_column
-    chosen = lax.all_gather(left_factor[:block_rows], "row", axis=0, tiled=True)
-    portion = chosen
-    summed = lax.psum_scatter(
-        jnp.einsum("pk,mk->pm", portion, left_factor, preferred_element_type=jnp.float32),
-        "col",
-        scatter_dimension=0,
-        tiled=True,
+    b = right_block.shape[0]
+    w = gram_panel.shape[1]
+    solved = lax.all_gather(solved_prev, "row", axis=0, tiled=True)
+    mine = lax.all_gather(left_factor[:b], "col", axis=1, tiled=True)
+    diagonal, low = updated(left_factor, gram_panel, b)
+    reduced = right_block - jnp.dot(mine, solved, preferred_element_type=jnp.float32)
+    reduced = lax.all_gather(reduced, "row", axis=0, tiled=True)
+    inverse = invert(diagonal)
+    top = lax.dynamic_slice_in_dim(diagonal, row_place * b, b, 0)
+    panel_factor = lax.dot_general(
+        jnp.concatenate([top, low], axis=0),
+        lax.dynamic_slice_in_dim(inverse, col_place * w, w, 0),
+        (((1,), (1,)), ((), ())),
+        precision=lax.Precision.HIGH,
     )
-    update = gram_panel - summed.T
-    diag_part = lax.all_gather(update[:block_rows], "row", axis=0, tiled=True)
-    diagonal = lax.all_gather(diag_part, "col", axis=1, tiled=True)
-    inverse = invert(diagonal)
-    inverse_cols = lax.dynamic_slice_in_dim(inverse, col_place * col_width, col_width, 0)
-    inverse_part = inverse_cols
-    panel_factor = lax.dot_general(
-        lax.all_gather(update, "col", axis=1, tiled=True),
-        inverse_part,
-        (((1,), (1,)), ((), ())),
-        precision=lax.Precision.HIGHEST,
-    )
-    strip_piece = lax.dynamic_slice_in_dim(
-        chosen, row_place % per_column * strip_width, strip_width, 1
-    )
-    strip_piece = spread(strip_piece, "col", row_place // per_column)
-    portion = strip_piece
-    reduced = right_block - lax.psum_scatter(
-        jnp.dot(portion, solved_prev, preferred_element_type=jnp.float32),
-        "row",
-        scatter_dimension=0,
-        tiled=True,
-    )
-    inverse_rows = lax.dynamic_slice_in_dim(inverse, row_place * block_rows, block_rows, 0)
-    inverse_part = inverse_rows
     solved_panel = jnp.dot(
-        inverse_part,
-        lax.all_gather(reduced, "row", axis=0, tiled=True),
-        precision=lax.Precision.HIGHEST,
+        lax.dynamic_slice_in_dim(inverse, row_place * b, b, 0),
+        reduced,
+        precision=lax.Precision.HIGH,
     )
     return (panel_factor, solved_panel)
 

time: 349 us -> 224 us (0.64); the launches traced: 348 us -> 220 us
  waiting for transfers between devices: 256 us -> 69.9 us
  Pallas kernels: 53.3 us -> 124 us
  matrix products: 13.9 us -> 8.44 us
  other arithmetic: 3.92 us -> 0 us
    pallas_call x0 -> x1, Pallas kernels: none -> 70.2 us  [updated(): pl.pallas_call(functools.partial(update_kernel, rows_n, cols_n), out_shap...]
    reduce_scatter x2 -> x0, waiting for transfers between devices: 69.5 us -> none  [the longest x1 43.5 us: body(): lax.psum_scatter(jnp.dot(portion, solved_prev, preferred_element_type=jnp...]
    all_gather x5 -> x3, waiting for transfers between devices: 134 us -> 69.2 us  [the longest x1 38.1 us: body(): solved = lax.all_gather(solved_prev, 'row', axis=0, tiled=True)]
    psum x1 -> x0, waiting for transfers between devices: 51.2 us -> none  [spread(): return lax.psum(kept, axis)]
    dot_general x4 -> x3, matrix products: 13.9 us -> 8.44 us  [the longest x1 3.94 us: body(): jnp.dot(mine, solved, preferred_element_type=jnp.float32)]
  transfers between devices with their start and end apart: 8 -> 3, of which waited for: 6 -> 2; matrix products, arithmetic and copies ran while one was open for 3% -> 1% of each run, Pallas kernels for 15% -> 56%
where the time goes in v2:
time: 224 us; the launch traced here: 220 us
  Pallas kernels  124 us (55%)
  waiting for transfers between devices  69.9 us (31%)
  between operations  13.8 us (6%)
  matrix products  8.44 us (4%)
  local copies, waits for them, and re-layouts  3.73 us (2%)
    pallas_call x1, Pallas kernels, updated(): pl.pallas_call(functools.partial(update_kernel, rows_n, cols_n), out_shap...  70.2 us
    pallas_call x1, Pallas kernels, invert(): pl.pallas_call(inverse_kernel, out_shape=jax.ShapeDtypeStruct((size, size...  53.3 us
    all_gather x1, waiting for transfers between devices, body(): solved = lax.all_gather(solved_prev, 'row', axis=0, tiled=True)  38.1 us
    all_gather x1, waiting for transfers between devices, body(): mine = lax.all_gather(left_factor[:b], 'col', axis=1, tiled=True)  31 us
  transfers between devices with their start and end apart: 3, of which 2 were waited for; matrix products, arithmetic and copies ran while one was open for 1% of the time, Pallas kernels for 56%

profile of v2, /device:TPU:0, one launch (start us, length us, event | category | flops | bytes accessed | tf_op | source)
XLA Modules:
  0.0 219.5 jit_solution(13286767059188116528)
XLA Ops:
  7.2 0.0 copy-start.1
  7.2 0.0 copy-start.2
  7.2 0.0 all-gather.4.cloned.1.call-start
  7.2 1.7 slice.3
  9.0 0.0 all-gather.4.cloned.1.call-update
  9.0 0.0 all-gather.6.cloned.1.call-start
  9.0 0.7 all-gather.6.cloned.1.call-update
  9.7 0.0 all-gather.8.cloned.1.call-start
  9.8 31.0 %all-gather.4.cloned.1.call-done = bf16[128,4096]{1,0:T(8,128)(2,1)} async-done(((bf16[128,1024]{1,0:T(8,128)(2,1)}), bf16[128,4096]{1,0:T(8,128)(2,1)}) %all-gather.4.cloned.1.call-update) | async-done | bytes 1048592 | tf_op jit(solution)/shard_map/all_gather | solution.py:309
  40.8 38.1 %all-gather.6.cloned.1.call-done = bf16[4096,512]{1,0:T(8,128)(2,1)} async-done(((bf16[512,512]{1,0:T(8,128)(2,1)}), bf16[4096,512]{1,0:T(8,128)(2,1)}) %all-gather.6.cloned.1.call-update) | async-done | bytes 4194320 | tf_op jit(solution)/shard_map/all_gather | solution.py:308
  79.0 3.9 %convolution_subtract_fusion = f32[128,512]{1,0:T(8,128)} fusion(f32[128,512]{1,0:T(8,128)} %param.7, bf16[128,4096]{1,0:T(8,128)(2,1)} %all-gather.4.cloned.1.call-done, bf16[4096,512]{1,0:T(8,128)(2,1)} %all-gather.6.cloned.1.call-done), kind=kOutput, calls=%fused_computation | convolution fusion | flops 536936448 | bytes 5767168 | tf_op jit(solution)/shard_map/dot_general | solution.py:311
  82.9 0.0 all-gather.8.cloned.1.call-update
  82.9 0.0 copy-done.1
  82.9 0.0 copy-done.2
  83.0 70.2 %shard_map.59 = (f32[1024,1024]{1,0:T(8,128)S(1)}, f32[128,1024]{1,0:T(8,128)S(1)}) custom-call(bf16[256,1024]{1,0:T(8,128)(2,1)S(1)} %copy-done.1, f32[256,256]{1,0:T(8,128)S(1)} %copy-done.2), custom_call_target="tpu_custom_call" | custom-call | flops 536870912 | bytes 8388608 | tf_op jit(solution)/shard_map/pallas_call | solution.py:283
  153.2 53.3 %shard_map.60 = f32[1024,1024]{1,0:T(8,128)S(1)} custom-call(f32[1024,1024]{1,0:T(8,128)S(1)} %get-tuple-element.4.d_ref), custom_call_target="tpu_custom_call" | custom-call | flops 4294967296 | bytes 8388608 | tf_op jit(solution)/shard_map/pallas_call | solution.py:97
  206.5 0.0 copy-start
  206.5 1.9 copy-done
  208.5 1.3 fusion
  209.8 0.0 all-gather.8.cloned.1.call-done
  209.8 3.2 %fusion.5 = f32[128,512]{1,0:T(8,128)} fusion(f32[1024,512]{1,0:T(8,128)} %all-gather.8.cloned.1.call-done, f32[1024,1024]{1,0:T(8,128)} %copy-done, s32[]{:T(128)S(6)} %select_n.7), kind=kOutput, calls=%fused_computation.6 | convolution fusion | flops 402653184 | bytes 2883588 | tf_op jit(solution)/shard_map/dot_general | solution.py:321
  (1 shorter events, 0.0 us)
Async XLA Ops:
  7.2 75.8 %copy-start.1 = (bf16[256,1024]{1,0:T(8,128)(2,1)S(1)}, bf16[256,1024]{1,0:T(8,128)(2,1)}, u32[]{:S(2)}) copy-start(bf16[256,1024]{1,0:T(8,128)(2,1)} %left_ref.1) | copy-start | bytes 1572868
  7.2 75.8 %copy-start.2 = (f32[256,256]{1,0:T(8,128)S(1)}, f32[256,256]{1,0:T(8,128)}, u32[]{:S(2)}) copy-start(f32[256,256]{1,0:T(8,128)} %gram_ref.1) | copy-start | bytes 786436
  7.2 33.6 %all-gather.4.cloned.1.call-start = ((), (), s32[]{:S(2)}) async-start(), calls=%async_computation | async-start | bytes 1310720 | tf_op jit(solution)/shard_map/all_gather | solution.py:309
  9.0 70.0 %all-gather.6.cloned.1.call-start = ((), (), s32[]{:S(2)}) async-start(), calls=%async_computation.1 | async-start | bytes 4718592 | tf_op jit(solution)/shard_map/all_gather | solution.py:308
  9.7 200.1 %all-gather.8.cloned.1.call-start = ((), (), s32[]{:S(2)}) async-start(), calls=%async_computation.2 | async-start | bytes 2359296 | tf_op jit(solution)/shard_map/all_gather | solution.py:312
  206.5 2.0 copy-start
Sparse Core Ops, SparseCore 0:
  10.2 30.6 all-gather.3
  42.7 36.1 all-gather.5
  83.0 30.7 all-gather.7

commit v3 on v2

--- a/solution.py
+++ b/solution.py
@@ -101,7 +101,7 @@
         out_specs=pl.BlockSpec(memory_space=pltpu.VMEM),
         scratch_shapes=[pltpu.VMEM((size, size), jnp.float32)],
         compiler_params=pltpu.CompilerParams(vmem_limit_bytes=40 * 1024 * 1024),
-        cost_estimate=pl.CostEstimate(flops=4 * size**3, bytes_accessed=8 * size * size, transcendentals=0),
+        cost_estimate=pl.CostEstimate(flops=4 * size**3, bytes_accessed=192 * size * size, transcendentals=0),
     )(diagonal)
 
 
@@ -296,7 +296,7 @@
         compiler_params=pltpu.CompilerParams(
             collective_id=0, has_side_effects=True, vmem_limit_bytes=48 * 1024 * 1024
         ),
-        cost_estimate=pl.CostEstimate(flops=2 * size * rows * 1024, bytes_accessed=8 * 1024 * 1024, transcendentals=0),
+        cost_estimate=pl.CostEstimate(flops=2 * size * rows * 1024, bytes_accessed=256 * size * size, transcendentals=0),
     )(left_factor, gram_panel)
 
 
@@ -308,6 +308,7 @@
     solved = lax.all_gather(solved_prev, "row", axis=0, tiled=True)
     mine = lax.all_gather(left_factor[:b], "col", axis=1, tiled=True)
     diagonal, low = updated(left_factor, gram_panel, b)
+    solved, mine, diagonal, low = lax.optimization_barrier((solved, mine, diagonal, low))
     reduced = right_block - jnp.dot(mine, solved, preferred_element_type=jnp.float32)
     reduced = lax.all_gather(reduced, "row", axis=0, tiled=True)
     inverse = invert(diagonal)

time: 224 us -> 185 us (0.83); the launches traced: 220 us -> 184 us
  waiting for transfers between devices: 69.9 us -> 10.8 us
  Pallas kernels: 124 us -> 140 us
  local copies, waits for them, and re-layouts: 3.73 us -> 10.8 us
    all_gather x1, waiting for transfers between devices: 31 us -> 0.01 us  [body(): mine = lax.all_gather(left_factor[:b], 'col', axis=1, tiled=True)]
    all_gather x1, waiting for transfers between devices: 38.1 us -> 10.1 us  [body(): solved = lax.all_gather(solved_prev, 'row', axis=0, tiled=True)]
    pallas_call x1, Pallas kernels: 70.2 us -> 87.2 us  [updated(): pl.pallas_call(functools.partial(update_kernel, rows_n, cols_n), out_shap...]
    unnamed x6 -> x10, local copies, waits for them, and re-layouts: 1.95 us -> 8.05 us
  transfers between devices with their start and end apart: 3 -> 3, of which waited for: 2 -> 1; matrix products, arithmetic and copies ran while one was open for 1% -> 1% of each run, Pallas kernels for 56% -> 76%
where the time goes in v3:
time: 185 us; the launch traced here: 184 us
  Pallas kernels  140 us (76%)
  between operations  13.8 us (7%)
  local copies, waits for them, and re-layouts  10.8 us (6%)
  waiting for transfers between devices  10.8 us (6%)
  matrix products  8.44 us (5%)
    pallas_call x1, Pallas kernels, updated(): pl.pallas_call(functools.partial(update_kernel, rows_n, cols_n), out_shap...  87.2 us
    pallas_call x1, Pallas kernels, invert(): pl.pallas_call(inverse_kernel, out_shape=jax.ShapeDtypeStruct((size, size...  53.3 us
    all_gather x1, waiting for transfers between devices, body(): solved = lax.all_gather(solved_prev, 'row', axis=0, tiled=True)  10.1 us
    unnamed x10, local copies, waits for them, and re-layouts  8.05 us
    dot_general x1, matrix products, body(): jnp.dot(mine, solved, preferred_element_type=jnp.float32)  3.95 us
  transfers between devices with their start and end apart: 3, of which 1 were waited for; matrix products, arithmetic and copies ran while one was open for 1% of the time, Pallas kernels for 76%

profile of v3, /device:TPU:0, one launch (start us, length us, event | category | flops | bytes accessed | tf_op | source)
XLA Modules:
  0.0 184.4 jit_solution(8998257844099846062)
XLA Ops:
  7.2 0.0 all-gather.6.cloned.1.call-start
  7.2 1.7 slice.3
  8.9 0.0 all-gather.6.cloned.1.call-update
  8.9 0.0 all-gather.4.cloned.1.call-start
  9.0 0.7 all-gather.4.cloned.1.call-update
  9.7 0.0 all-gather.8.cloned.1.call-start
  9.7 0.0 copy-start.1
  9.7 1.0 copy-done.1
  10.7 0.0 copy-start.4
  10.8 0.9 copy-done.4
  11.7 87.2 %shard_map.59 = (f32[1024,1024]{1,0:T(8,128)S(1)}, f32[128,1024]{1,0:T(8,128)S(1)}) custom-call(bf16[256,1024]{1,0:T(8,128)(2,1)S(1)} %copy-done.1, f32[256,256]{1,0:T(8,128)S(1)} %copy-done.4), custom_call_target="tpu_custom_call" | custom-call | flops 536870912 | bytes 268435456 | tf_op jit(solution)/shard_map/pallas_call | solution.py:283
  98.9 0.0 copy-start.2
  98.9 1.9 %copy-done.2 = f32[1024,1024]{1,0:T(8,128)} copy-done((f32[1024,1024]{1,0:T(8,128)}, f32[1024,1024]{1,0:T(8,128)S(1)}, u32[]{:S(2)}) %copy-start.2) | copy-done | bytes 4194328
  100.8 0.0 all-gather.6.cloned.1.call-done
  100.8 10.1 %all-gather.4.cloned.1.call-done = bf16[4096,512]{1,0:T(8,128)(2,1)} async-done(((bf16[512,512]{1,0:T(8,128)(2,1)}), bf16[4096,512]{1,0:T(8,128)(2,1)}) %all-gather.4.cloned.1.call-update) | async-done | bytes 4194320 | tf_op jit(solution)/shard_map/all_gather | solution.py:308
  110.9 3.9 %convolution_subtract_fusion = f32[128,512]{1,0:T(8,128)} fusion(f32[128,512]{1,0:T(8,128)} %param.7, bf16[128,4096]{1,0:T(8,128)(2,1)} %all-gather.6.cloned.1.call-done, bf16[4096,512]{1,0:T(8,128)(2,1)} %all-gather.4.cloned.1.call-done), kind=kOutput, calls=%fused_computation | convolution fusion | flops 536936448 | bytes 5767168 | tf_op jit(solution)/shard_map/dot_general | solution.py:312
  114.8 0.0 all-gather.8.cloned.1.call-update
  114.9 1.1 constant_dynamic-slice_fusion
  115.9 0.0 copy-start.3
  116.0 2.2 %copy-done.3 = f32[1024,1024]{1,0:T(8,128)S(1)} copy-done((f32[1024,1024]{1,0:T(8,128)S(1)}, f32[1024,1024]{1,0:T(8,128)}, u32[]{:S(2)}) %copy-start.3) | copy-done | bytes 4194328
  118.1 53.3 %shard_map.60 = f32[1024,1024]{1,0:T(8,128)S(1)} custom-call(f32[1024,1024]{1,0:T(8,128)S(1)} %copy-done.3), custom_call_target="tpu_custom_call" | custom-call | flops 4294967296 | bytes 201326592 | tf_op jit(solution)/shard_map/pallas_call | solution.py:97
  171.4 0.0 copy-start
  171.5 1.9 %copy-done = f32[1024,1024]{1,0:T(8,128)} copy-done((f32[1024,1024]{1,0:T(8,128)}, f32[1024,1024]{1,0:T(8,128)S(1)}, u32[]{:S(2)}) %copy-start) | copy-done | bytes 4194328
  173.4 1.3 fusion
  174.7 0.0 all-gather.8.cloned.1.call-done
  174.7 3.2 %fusion.5 = f32[128,512]{1,0:T(8,128)} fusion(f32[1024,512]{1,0:T(8,128)} %all-gather.8.cloned.1.call-done, f32[1024,1024]{1,0:T(8,128)} %copy-done, s32[]{:T(128)S(6)} %select_n.7), kind=kOutput, calls=%fused_computation.6 | convolution fusion | flops 402653184 | bytes 2883588 | tf_op jit(solution)/shard_map/dot_general | solution.py:322
Async XLA Ops:
  7.2 93.6 %all-gather.6.cloned.1.call-start = ((), (), s32[]{:S(2)}) async-start(), calls=%async_computation.1 | async-start | bytes 1310720 | tf_op jit(solution)/shard_map/all_gather | solution.py:309
  8.9 102.0 %all-gather.4.cloned.1.call-start = ((), (), s32[]{:S(2)}) async-start(), calls=%async_computation | async-start | bytes 4718592 | tf_op jit(solution)/shard_map/all_gather | solution.py:308
  9.7 165.1 %all-gather.8.cloned.1.call-start = ((), (), s32[]{:S(2)}) async-start(), calls=%async_computation.2 | async-start | bytes 2359296 | tf_op jit(solution)/shard_map/all_gather | solution.py:313
  9.7 1.0 copy-start.1
  10.7 0.9 copy-start.4
  98.9 1.9 %copy-start.2 = (f32[1024,1024]{1,0:T(8,128)}, f32[1024,1024]{1,0:T(8,128)S(1)}, u32[]{:S(2)}) copy-start(f32[1024,1024]{1,0:T(8,128)S(1)} %get-tuple-element.10.d_ref) | copy-start | bytes 12582916
  115.9 2.2 %copy-start.3 = (f32[1024,1024]{1,0:T(8,128)S(1)}, f32[1024,1024]{1,0:T(8,128)}, u32[]{:S(2)}) copy-start(f32[1024,1024]{1,0:T(8,128)} %copy-done.2) | copy-start | bytes 12582916
  171.4 1.9 %copy-start = (f32[1024,1024]{1,0:T(8,128)}, f32[1024,1024]{1,0:T(8,128)S(1)}, u32[]{:S(2)}) copy-start(f32[1024,1024]{1,0:T(8,128)S(1)} %shard_map.60) | copy-start | bytes 12582916
Sparse Core Ops, SparseCore 0:
  10.1 43.3 all-gather.5
  55.5 55.3 all-gather.3
  115.0 28.1 all-gather.7

commit v4 on v3

--- a/solution.py
+++ b/solution.py
@@ -25,35 +25,57 @@
     return lax.dot_general(a, b, (dims, ((), ())), preferred_element_type=jnp.float32)
 
 
+def reciprocal(value):
+    guess = pl.reciprocal(value, approx=True)
+    return guess * (2.0 - value * guess)
+
+
+def spread_row(value, j):
+    return jnp.broadcast_to(value[j : j + 1], (STRIP, TILE))
+
+
+def spread_lane(value, k):
+    return jnp.broadcast_to(value[:, k : k + 1], (STRIP, TILE))
+
+
 def invert_tile(a):
     lane = lax.broadcasted_iota(jnp.int32, (STRIP, TILE), 1)
     sub = lax.broadcasted_iota(jnp.int32, (STRIP, TILE), 0)
     lane_all = lax.broadcasted_iota(jnp.int32, (TILE, TILE), 1)
     done = []
+    strip, below = a[:STRIP], a[STRIP:]
     for g in range(TILE // STRIP):
         lo = g * STRIP
-        strip = a[:STRIP]
-        cols = [
-            jnp.broadcast_to(strip[:, lo + k : lo + k + 1], (STRIP, TILE)) for k in range(STRIP)
-        ]
-        t = jnp.where((lane >= lo) & (lane < lo + STRIP), (lane - lo == sub).astype(jnp.float32), strip)
+        hi = lo + STRIP
+        cols = [spread_lane(strip, lo + k) for k in range(STRIP)]
+        t = jnp.where((lane >= lo) & (lane < hi), (lane - lo == sub).astype(jnp.float32), strip)
         out = jnp.zeros_like(t)
-        for j in range(STRIP):
-            pivot = jnp.broadcast_to(cols[j][j : j + 1], (STRIP, TILE))
-            inv = 1.0 / pivot
-            row = jnp.broadcast_to(t[j : j + 1], (STRIP, TILE))
-            out = jnp.where(sub == j, row * lax.rsqrt(pivot), out)
-            mult = jnp.where(sub == j, 1.0 - inv, cols[j] * inv)
-            t = t - mult * row
-            for k in range(j + 1, STRIP):
-                cols[k] = cols[k] - mult * jnp.broadcast_to(cols[k][j : j + 1], (STRIP, TILE))
-        done.append(jnp.where(lane < lo + STRIP, out, 0.0))
-        if lo + STRIP < TILE:
-            below = a[STRIP:]
-            rows = TILE - lo - STRIP
-            inside = (lane_all[:rows] >= lo) & (lane_all[:rows] < lo + STRIP)
-            sent = strip.T[lo + STRIP :]
-            a = jnp.where(inside, 0.0, below) - dot3(sent, t)
+        for j in range(0, STRIP, 2):
+            p11, p12, p22 = spread_row(cols[j], j), spread_row(cols[j + 1], j), spread_row(cols[j + 1], j + 1)
+            det = p11 * p22 - p12 * p12
+            inv = reciprocal(det)
+            row1, row2 = spread_row(t, j), spread_row(t, j + 1)
+            root = lax.rsqrt(p11)
+            out = jnp.where(sub == j, row1 * root, out)
+            out = jnp.where(sub == j + 1, (row2 * p11 - row1 * p12) * (root * lax.rsqrt(det)), out)
+            one = (cols[j] * p22 - cols[j + 1] * p12) * inv
+            two = (cols[j + 1] * p11 - cols[j] * p12) * inv
+            cross = p12 * inv
+            one = jnp.where(sub == j, 1.0 - p22 * inv, jnp.where(sub == j + 1, cross, one))
+            two = jnp.where(sub == j, cross, jnp.where(sub == j + 1, 1.0 - p11 * inv, two))
+            t = t - one * row1 - two * row2
+            for k in range(j + 2, STRIP):
+                cols[k] = cols[k] - one * spread_row(cols[k], j) - two * spread_row(cols[k], j + 1)
+        done.append(jnp.where(lane < hi, out, 0.0))
+        if hi < TILE:
+            sent = strip.T[hi:]
+            strip = jnp.where((lane >= lo) & (lane < hi), 0.0, below[:STRIP])
+            for k in range(STRIP):
+                strip = strip - spread_lane(sent[:STRIP], k) * spread_row(t, k)
+            if hi + STRIP < TILE:
+                inside = lane_all[: TILE - hi - STRIP]
+                inside = (inside >= lo) & (inside < hi)
+                below = jnp.where(inside, 0.0, below[STRIP:]) - dot3(sent[STRIP:], t)
     return jnp.concatenate(done, axis=0)
 
 

time: 185 us -> 175 us (0.946)
  Pallas kernels: 140 us -> 131 us
    pallas_call x1, Pallas kernels: 53.3 us -> 43.9 us  [invert(): pl.pallas_call(inverse_kernel, out_shape=jax.ShapeDtypeStruct((size, size...]
  transfers between devices with their start and end apart: 3 -> 3, of which waited for: 1 -> 1; matrix products, arithmetic and copies ran while one was open for 1% -> 1% of each run, Pallas kernels for 76% -> 75%
where the time goes in v4:
time: 175 us
  Pallas kernels  131 us (75%)
  between operations  13.8 us (8%)
  local copies, waits for them, and re-layouts  10.8 us (6%)
  waiting for transfers between devices  10.8 us (6%)
  matrix products  8.44 us (5%)
    pallas_call x1, Pallas kernels, updated(): pl.pallas_call(functools.partial(update_kernel, rows_n, cols_n), out_shap...  87.2 us
    pallas_call x1, Pallas kernels, invert(): pl.pallas_call(inverse_kernel, out_shape=jax.ShapeDtypeStruct((size, size...  43.9 us
    all_gather x1, waiting for transfers between devices, body(): solved = lax.all_gather(solved_prev, 'row', axis=0, tiled=True)  10.1 us
    unnamed x10, local copies, waits for them, and re-layouts  8.05 us
    dot_general x1, matrix products, body(): jnp.dot(mine, solved, preferred_element_type=jnp.float32)  3.95 us
  transfers between devices with their start and end apart: 3, of which 1 were waited for; matrix products, arithmetic and copies ran while one was open for 1% of the time, Pallas kernels for 75%

profile of v4, /device:TPU:0, one launch (start us, length us, event | category | flops | bytes accessed | tf_op | source)
XLA Modules:
  0.0 175.0 jit_solution(7429571777706832700)
XLA Ops:
  7.2 0.0 all-gather.6.cloned.1.call-start
  7.2 1.7 slice.3
  8.9 0.0 all-gather.6.cloned.1.call-update
  8.9 0.0 all-gather.4.cloned.1.call-start
  9.0 0.7 all-gather.4.cloned.1.call-update
  9.7 0.0 all-gather.8.cloned.1.call-start
  9.7 0.0 copy-start.1
  9.7 1.0 copy-done.1
  10.7 0.0 copy-start.4
  10.8 0.9 copy-done.4
  11.7 87.2 %shard_map.59 = (f32[1024,1024]{1,0:T(8,128)S(1)}, f32[128,1024]{1,0:T(8,128)S(1)}) custom-call(bf16[256,1024]{1,0:T(8,128)(2,1)S(1)} %copy-done.1, f32[256,256]{1,0:T(8,128)S(1)} %copy-done.4), custom_call_target="tpu_custom_call" | custom-call | flops 536870912 | bytes 268435456 | tf_op jit(solution)/shard_map/pallas_call | solution.py:305
  98.9 0.0 copy-start.2
  98.9 1.9 %copy-done.2 = f32[1024,1024]{1,0:T(8,128)} copy-done((f32[1024,1024]{1,0:T(8,128)}, f32[1024,1024]{1,0:T(8,128)S(1)}, u32[]{:S(2)}) %copy-start.2) | copy-done | bytes 4194328
  100.8 0.0 all-gather.6.cloned.1.call-done
  100.8 10.1 %all-gather.4.cloned.1.call-done = bf16[4096,512]{1,0:T(8,128)(2,1)} async-done(((bf16[512,512]{1,0:T(8,128)(2,1)}), bf16[4096,512]{1,0:T(8,128)(2,1)}) %all-gather.4.cloned.1.call-update) | async-done | bytes 4194320 | tf_op jit(solution)/shard_map/all_gather | solution.py:330
  110.9 3.9 %convolution_subtract_fusion = f32[128,512]{1,0:T(8,128)} fusion(f32[128,512]{1,0:T(8,128)} %param.7, bf16[128,4096]{1,0:T(8,128)(2,1)} %all-gather.6.cloned.1.call-done, bf16[4096,512]{1,0:T(8,128)(2,1)} %all-gather.4.cloned.1.call-done), kind=kOutput, calls=%fused_computation | convolution fusion | flops 536936448 | bytes 5767168 | tf_op jit(solution)/shard_map/dot_general | solution.py:334
  114.8 0.0 all-gather.8.cloned.1.call-update
  114.9 1.1 constant_dynamic-slice_fusion
  115.9 0.0 copy-start.3
  116.0 2.2 %copy-done.3 = f32[1024,1024]{1,0:T(8,128)S(1)} copy-done((f32[1024,1024]{1,0:T(8,128)S(1)}, f32[1024,1024]{1,0:T(8,128)}, u32[]{:S(2)}) %copy-start.3) | copy-done | bytes 4194328
  118.1 43.9 %shard_map.60 = f32[1024,1024]{1,0:T(8,128)S(1)} custom-call(f32[1024,1024]{1,0:T(8,128)S(1)} %copy-done.3), custom_call_target="tpu_custom_call" | custom-call | flops 4294967296 | bytes 201326592 | tf_op jit(solution)/shard_map/pallas_call | solution.py:119
  162.0 0.0 copy-start
  162.0 1.9 %copy-done = f32[1024,1024]{1,0:T(8,128)} copy-done((f32[1024,1024]{1,0:T(8,128)}, f32[1024,1024]{1,0:T(8,128)S(1)}, u32[]{:S(2)}) %copy-start) | copy-done | bytes 4194328
  164.0 1.3 fusion
  165.3 0.0 all-gather.8.cloned.1.call-done
  165.3 3.2 %fusion.5 = f32[128,512]{1,0:T(8,128)} fusion(f32[1024,512]{1,0:T(8,128)} %all-gather.8.cloned.1.call-done, f32[1024,1024]{1,0:T(8,128)} %copy-done, s32[]{:T(128)S(6)} %select_n.7), kind=kOutput, calls=%fused_computation.6 | convolution fusion | flops 402653184 | bytes 2883588 | tf_op jit(solution)/shard_map/dot_general | solution.py:344
Async XLA Ops:
  7.2 93.6 %all-gather.6.cloned.1.call-start = ((), (), s32[]{:S(2)}) async-start(), calls=%async_computation.1 | async-start | bytes 1310720 | tf_op jit(solution)/shard_map/all_gather | solution.py:331
  8.9 102.0 %all-gather.4.cloned.1.call-start = ((), (), s32[]{:S(2)}) async-start(), calls=%async_computation | async-start | bytes 4718592 | tf_op jit(solution)/shard_map/all_gather | solution.py:330
  9.7 155.6 %all-gather.8.cloned.1.call-start = ((), (), s32[]{:S(2)}) async-start(), calls=%async_computation.2 | async-start | bytes 2359296 | tf_op jit(solution)/shard_map/all_gather | solution.py:335
  9.7 1.0 copy-start.1
  10.7 0.9 copy-start.4
  98.9 1.9 %copy-start.2 = (f32[1024,1024]{1,0:T(8,128)}, f32[1024,1024]{1,0:T(8,128)S(1)}, u32[]{:S(2)}) copy-start(f32[1024,1024]{1,0:T(8,128)S(1)} %get-tuple-element.10.d_ref) | copy-start | bytes 12582916
  115.9 2.2 %copy-start.3 = (f32[1024,1024]{1,0:T(8,128)S(1)}, f32[1024,1024]{1,0:T(8,128)}, u32[]{:S(2)}) copy-start(f32[1024,1024]{1,0:T(8,128)} %copy-done.2) | copy-start | bytes 12582916
  162.0 1.9 %copy-start = (f32[1024,1024]{1,0:T(8,128)}, f32[1024,1024]{1,0:T(8,128)S(1)}, u32[]{:S(2)}) copy-start(f32[1024,1024]{1,0:T(8,128)S(1)} %shard_map.60) | copy-start | bytes 12582916
Sparse Core Ops, SparseCore 0:
  10.1 43.3 all-gather.5
  55.5 55.3 all-gather.3
  115.0 27.9 all-gather.7

commit v5 on v4

v5 whole, which is shorter than its diff:
```python
import functools

import jax
import jax.numpy as jnp
from jax import lax
from jax.experimental import pallas as pl
from jax.experimental.pallas import tpu as pltpu
from jax.sharding import PartitionSpec as P

STRIP = 8
TILE = 128


def halves(value):
    high = value.astype(jnp.bfloat16)
    low = (value - high.astype(jnp.float32)).astype(jnp.bfloat16)
    return high, low


def dot3(left, right, dims=((1,), (0,))):
    lh, ll = halves(left)
    rh, rl = halves(right)
    a = jnp.concatenate([lh, lh, ll], axis=dims[0][0])
    b = jnp.concatenate([rh, rl, rh], axis=dims[1][0])
    return lax.dot_general(a, b, (dims, ((), ())), preferred_element_type=jnp.float32)


def reciprocal(value):
    guess = pl.reciprocal(value, approx=True)
    return guess * (2.0 - value * guess)


def spread_row(value, j):
    return jnp.broadcast_to(value[j : j + 1], (STRIP, TILE))


def spread_lane(value, k):
    return jnp.broadcast_to(value[:, k : k + 1], (STRIP, TILE))


def invert_tile(a):
    lane = lax.broadcasted_iota(jnp.int32, (STRIP, TILE), 1)
    sub = lax.broadcasted_iota(jnp.int32, (STRIP, TILE), 0)
    lane_all = lax.broadcasted_iota(jnp.int32, (TILE, TILE), 1)
    done = []
    strip, below = a[:STRIP], a[STRIP:]
    for g in range(TILE // STRIP):
        lo = g * STRIP
        hi = lo + STRIP
        cols = [spread_lane(strip, lo + k) for k in range(STRIP)]
        t = jnp.where((lane >= lo) & (lane < hi), (lane - lo == sub).astype(jnp.float32), strip)
        out = jnp.zeros_like(t)
        for j in range(0, STRIP, 2):
            p11, p12, p22 = spread_row(cols[j], j), spread_row(cols[j + 1], j), spread_row(cols[j + 1], j + 1)
            det = p11 * p22 - p12 * p12
            inv = reciprocal(det)
            row1, row2 = spread_row(t, j), spread_row(t, j + 1)
            root = lax.rsqrt(p11)
            out = jnp.where(sub == j, row1 * root, out)
            out = jnp.where(sub == j + 1, (row2 * p11 - row1 * p12) * (root * lax.rsqrt(det)), out)
            one = (cols[j] * p22 - cols[j + 1] * p12) * inv
            two = (cols[j + 1] * p11 - cols[j] * p12) * inv
            cross = p12 * inv
            one = jnp.where(sub == j, 1.0 - p22 * inv, jnp.where(sub == j + 1, cross, one))
            two = jnp.where(sub == j, cross, jnp.where(sub == j + 1, 1.0 - p11 * inv, two))
            t = t - one * row1 - two * row2
            for k in range(j + 2, STRIP):
                cols[k] = cols[k] - one * spread_row(cols[k], j) - two * spread_row(cols[k], j + 1)
        done.append(jnp.where(lane < hi, out, 0.0))
        if hi < TILE:
            sent = strip.T[hi:]
            strip = jnp.where((lane >= lo) & (lane < hi), 0.0, below[:STRIP])
            for k in range(STRIP):
                strip = strip - spread_lane(sent[:STRIP], k) * spread_row(t, k)
            if hi + STRIP < TILE:
                inside = lane_all[: TILE - hi - STRIP]
                inside = (inside >= lo) & (inside < hi)
                below = jnp.where(inside, 0.0, below[STRIP:]) - dot3(sent[STRIP:], t)
    return jnp.concatenate(done, axis=0)


def inverse_kernel(d_ref, o_ref, w_ref):
    pieces, size, width = d_ref.shape
    count = size // TILE
    for q in range(pieces):
        w_ref[:, q * width : (q + 1) * width] = d_ref[q]
    lane = lax.broadcasted_iota(jnp.int32, (TILE, size), 1)
    eye = (
        lax.broadcasted_iota(jnp.int32, (TILE, TILE), 0)
        == lax.broadcasted_iota(jnp.int32, (TILE, TILE), 1)
    ).astype(jnp.float32)

    def step(k, carry):
        at = pl.multiple_of(k * TILE, TILE)
        here = pl.ds(at, TILE)
        small = invert_tile(w_ref[here, here])
        w_ref[here, here] = eye
        z = dot3(small, w_ref[here, :])
        o_ref[here, :] = jnp.where(lane < at + TILE, z, 0.0)
        w_ref[here, :] = z
        zh, zl = halves(z)
        right = jnp.concatenate([zh, zl, zh], axis=0)

        def trail(i, c):
            mine = pl.ds(pl.multiple_of(i * TILE, TILE), TILE)
            yh, yl = halves(w_ref[here, mine].T)
            left = jnp.concatenate([yh, yh, yl], axis=1)
            w_ref[mine, here] = jnp.zeros((TILE, TILE), jnp.float32)
            w_ref[mine, :] -= jnp.dot(left, right, preferred_element_type=jnp.float32)
            return c

        lax.fori_loop(k + 1, count, trail, 0)
        return carry

    lax.fori_loop(0, count, step, 0)


def invert(diagonal):
    size = diagonal.shape[1]
    return pl.pallas_call(
        inverse_kernel,
        out_shape=jax.ShapeDtypeStruct((size, size), jnp.float32),
        in_specs=[pl.BlockSpec(memory_space=pltpu.VMEM)],
        out_specs=pl.BlockSpec(memory_space=pltpu.VMEM),
        scratch_shapes=[pltpu.VMEM((size, size), jnp.float32)],
        compiler_params=pltpu.CompilerParams(vmem_limit_bytes=40 * 1024 * 1024),
        cost_estimate=pl.CostEstimate(flops=4 * size**3, bytes_accessed=192 * size * size, transcendentals=0),
    )(diagonal)


MESH = pl.DeviceIdType.MESH


def copy(src, dst, send, recv, to):
    return pltpu.make_async_remote_copy(
        src_ref=src, dst_ref=dst, send_sem=send, recv_sem=recv, device_id=to, device_id_type=MESH
    )


class Place:
    def __init__(self, rows_n, cols_n):
        self.cols_n = cols_n
        self.pair = rows_n // cols_n
        self.chips = rows_n // self.pair
        self.r = lax.axis_index("row")
        self.c = lax.axis_index("col")
        self.core = self.r % self.pair
        self.p = self.r // self.pair
        self.sibling = (self.p * self.pair + (self.pair - 1 - self.core), self.c)

    def peer(self, s):
        return (((self.p + s) % self.chips) * self.pair + self.core, self.c)

    def origin(self, s):
        return (self.p + self.chips - s) % self.chips


class RowGather:
    def __init__(self, at, own, block, send, recv, side_send, side_recv):
        self.at, self.own, self.block = at, own, block
        self.send, self.recv, self.side_send, self.side_recv = send, recv, side_send, side_recv

    def far(self, s):
        at = self.at
        return copy(self.own, self.block(at.r), self.send(s), self.recv(s), at.peer(s))

    def far_in(self, s):
        at = self.at
        block = self.block(at.origin(s) * at.pair + at.core)
        return copy(block, block, self.send(s), self.recv(s), at.peer(s))

    def near(self, s):
        at = self.at
        block = self.block(at.origin(s) * at.pair + at.core)
        src = self.own if s == 0 else block
        return copy(src, block, self.side_send(s), self.side_recv(s), at.sibling)

    def near_in(self, s):
        at = self.at
        block = self.block(at.origin(s) * at.pair + (at.pair - 1 - at.core))
        return copy(block, block, self.side_send(s), self.side_recv(s), at.sibling)

    def start(self):
        for s in range(1, self.at.chips):
            self.far(s).start()
        self.near(0).start()

    def relay(self, s):
        if s > 0:
            self.far_in(s).wait_recv()
            self.near(s).start()

    def relay_all(self):
        for s in range(1, self.at.chips):
            self.relay(s)

    def arrive(self):
        for s in range(self.at.chips):
            self.near_in(s).wait_recv()

    def finish(self):
        for s in range(self.at.chips):
            if s > 0:
                self.far(s).wait_send()
            self.near(s).wait_send()


class ColGather:
    def __init__(self, at, block, send, recv):
        self.at, self.block, self.send, self.recv = at, block, send, recv

    def hop(self, way, t):
        at = self.at
        step = 1 if way == 0 else -1
        block = self.block(at.c - step * t)
        return copy(block, block, self.send.at[way, t], self.recv.at[way, t + 1], (at.r, at.c + step))

    def hop_in(self, way, t):
        at = self.at
        step = 1 if way == 0 else -1
        block = self.block(at.c - step * t)
        return copy(block, block, self.send.at[way, t], self.recv.at[way, t], (at.r, at.c - step))

    def has(self, way, t):
        return self.at.c >= t if way == 0 else self.at.c < self.at.cols_n - t

    def goes(self, way):
        return self.has(1 - way, 1)

    def start(self):
        for way in range(2):
            pl.when(self.goes(way))(self.hop(way, 0).start)

    def take(self, t, use=None):
        for way in range(2):

            @pl.when(self.has(way, t))
            def _(way=way):
                self.hop_in(way, t).wait_recv()
                if t + 1 < self.at.cols_n:
                    pl.when(self.goes(way))(self.hop(way, t).start)
                if use is not None:
                    use(self.at.c - t if way == 0 else self.at.c + t)

    def finish(self):
        for way in range(2):
            for t in range(self.at.cols_n - 1):
                pl.when(self.has(way, t) & self.goes(way))(self.hop(way, t).wait_send)


def update_kernel(
    rows_n, cols_n, left_ref, gram_ref, solved_ref, right_ref, d_ref, rows_ref, reduced_ref,
    chosen, solved, mine, top_out, top_in, low_out, low_in, low_all,
    c_send, c_recv, cs_send, cs_recv, v_send, v_recv, vs_send, vs_recv,
    t_send, t_recv, l_send, l_recv, z_send, z_recv, y_send, y_recv, m_send, m_recv,
    d_send, d_recv, ds_send, ds_recv,
):
    at = Place(rows_n, cols_n)
    r, c, chips = at.r, at.c, at.chips
    b, w = right_ref.shape[0], low_all.shape[2]
    deep = solved_ref.shape[0]

    barrier = pltpu.get_barrier_semaphore()
    for s in range(1, chips):
        pl.semaphore_signal(barrier, inc=1, device_id=at.peer(s), device_id_type=MESH)
    for u in range(1, cols_n):
        pl.semaphore_signal(barrier, inc=1, device_id=(r, (c + u) % cols_n), device_id_type=MESH)
    pl.semaphore_signal(barrier, inc=1, device_id=at.sibling, device_id_type=MESH)
    pl.semaphore_wait(barrier, chips + cols_n - 1)

    def span(q, size):
        return pl.ds(pl.multiple_of(q * size, size), size)

    def sems(*refs):
        return [lambda s, ref=ref: ref.at[s] for ref in refs]

    def to_owner(q, out, into, send, recv):
        return copy(out.at[q], into.at[c], send.at[q], recv.at[c], (r, q))

    def from_owner(q, out, into, send, recv):
        return copy(out.at[q], into.at[q], send.at[q], recv.at[q], (r, q))

    def product(rows, q):
        return lax.dot_general(
            rows, chosen[span(q, w), :], (((1,), (1,)), ((), ())), preferred_element_type=jnp.float32
        )

    def total(start, out, into, pair):
        value = start - out[c]
        for u in range(1, cols_n):
            q = (c + u) % cols_n
            from_owner(q, out, into, *pair).wait_recv()
            value = value - into[q]
        return value

    def piece(q):
        return RowGather(
            at, d_ref.at[q, span(r, b)], lambda i: d_ref.at[q, span(i, b)],
            *[lambda s, ref=ref: ref.at[q, s] for ref in (d_send, d_recv, ds_send, ds_recv)]
        )

    def pieces(t, act):
        if t == 0:
            act(piece(c))
        else:
            pl.when(c >= t)(lambda: act(piece(c - t)))
            pl.when(c < cols_n - t)(lambda: act(piece(c + t)))

    top_sems, low_sems = (t_send, t_recv), (l_send, l_recv)
    first = RowGather(
        at, left_ref.at[pl.ds(0, b)], lambda i: chosen.at[span(i, b)], *sems(c_send, c_recv, cs_send, cs_recv)
    )
    second = RowGather(
        at, solved_ref, lambda i: solved.at[span(i, deep)], *sems(v_send, v_recv, vs_send, vs_recv)
    )

    def sent(s):
        first.near_in(s).wait_recv()
        q = at.origin(s)
        top_out[q] = product(left_ref[:b], q)
        pl.when(q != c)(lambda: to_owner(q, top_out, top_in, *top_sems).start())

    first.start()
    chosen[span(r, b), :] = left_ref[:b]
    for s in range(chips):
        first.relay(s)
        if s != 1:
            sent(max(s - 1, 0))
    second.start()
    sent(chips - 1)
    mine[c] = left_ref[:b]
    solved[span(r, deep), :] = solved_ref[...]
    for s in range(chips):
        low_out[at.origin(s)] = product(left_ref[b:], at.origin(s))

    across = ColGather(at, lambda q: d_ref.at[q, span(r, b)], z_send, z_recv)
    others = ColGather(at, lambda q: mine.at[q], m_send, m_recv)
    lows = ColGather(at, lambda q: low_all.at[q], y_send, y_recv)
    d_ref[c, span(r, b), :] = total(gram_ref[:b], top_out, top_in, top_sems)
    across.start()
    piece(c).start()
    for u in range(1, cols_n):
        to_owner((c + u) % cols_n, low_out, low_in, *low_sems).start()
    for t in range(1, cols_n):
        across.take(t, lambda q: piece(q).start())
        if t == 1:
            others.start()
        pieces(t - 1, lambda part: part.relay_all())
    low_all[c] = total(gram_ref[b:], low_out, low_in, low_sems)
    lows.start()
    for t in range(1, cols_n):
        others.take(t)
        second.relay(t)
        lows.take(t)
    pieces(cols_n - 1, lambda part: part.relay_all())
    second.arrive()
    for q in range(cols_n):
        rows_ref[:b, q * w : (q + 1) * w] = d_ref[q, span(r, b), :]
        rows_ref[b:, q * w : (q + 1) * w] = low_all[q]
    value = right_ref[...]
    for i in range(rows_n):
        half = i % at.pair
        value = value - jnp.dot(
            mine[i // at.pair, :, half * deep : (half + 1) * deep],
            solved[i * deep : (i + 1) * deep, :],
            preferred_element_type=jnp.float32,
        )
    reduced_ref[...] = value
    for t in range(cols_n):
        pieces(t, lambda part: part.arrive())
    for t in range(cols_n):
        pieces(t, lambda part: part.finish())
    first.finish()
    second.finish()
    across.finish()
    others.finish()
    lows.finish()
    for u in range(1, cols_n):
        q = (c + u) % cols_n
        to_owner(q, top_out, top_in, *top_sems).wait_send()
        to_owner(q, low_out, low_in, *low_sems).wait_send()


def updated(left_factor, gram_panel, solved_prev, right_block):
    rows_n, cols_n = lax.axis_size("row"), lax.axis_size("col")
    rows, w = gram_panel.shape
    b, wide = right_block.shape
    size = rows_n * b
    f32, bf16 = jnp.float32, jnp.bfloat16
    vmem = pl.BlockSpec(memory_space=pltpu.VMEM)
    line = pltpu.SemaphoreType.DMA((cols_n,))
    ways = pltpu.SemaphoreType.DMA((2, cols_n))
    square = pltpu.SemaphoreType.DMA((cols_n, cols_n))
    return pl.pallas_call(
        functools.partial(update_kernel, rows_n, cols_n),
        out_shape=(
            jax.ShapeDtypeStruct((cols_n, size, w), f32),
            jax.ShapeDtypeStruct((rows, size), f32),
            jax.ShapeDtypeStruct((b, wide), f32),
        ),
        in_specs=[vmem] * 4,
        out_specs=(vmem,) * 3,
        scratch_shapes=[
            pltpu.VMEM((size, left_factor.shape[1]), bf16),
            pltpu.VMEM((rows_n * solved_prev.shape[0], wide), bf16),
            pltpu.VMEM((cols_n, b, left_factor.shape[1]), bf16),
        ]
        + [pltpu.VMEM((cols_n, b, w), f32)] * 2
        + [pltpu.VMEM((cols_n, rows - b, w), f32)] * 3
        + [line] * 12
        + [ways] * 6
        + [square] * 4,
        compiler_params=pltpu.CompilerParams(
            collective_id=0, has_side_effects=True, vmem_limit_bytes=52 * 1024 * 1024
        ),
        cost_estimate=pl.CostEstimate(flops=2 * size * rows * 1024, bytes_accessed=192 * size * size, transcendentals=0),
    )(left_factor, gram_panel, solved_prev, right_block)


def body(gram_panel, left_factor, solved_prev, right_block):
    row_place = lax.axis_index("row")
    col_place = lax.axis_index("col")
    b = right_block.shape[0]
    w = gram_panel.shape[1]
    diagonal, update, reduced = updated(left_factor, gram_panel, solved_prev, right_block)
    reduced = lax.all_gather(reduced, "row", axis=0, tiled=True)
    inverse = invert(diagonal)
    panel_factor = lax.dot_general(
        update,
        lax.dynamic_slice_in_dim(inverse, col_place * w, w, 0),
        (((1,), (1,)), ((), ())),
        precision=lax.Precision.HIGH,
    )
    solved_panel = jnp.dot(
        lax.dynamic_slice_in_dim(inverse, row_place * b, b, 0),
        reduced,
        precision=lax.Precision.HIGH,
    )
    return (panel_factor, solved_panel)


def solution(mesh):
    in_specs = (P("row", "col"), P("row", "col"), P("row", "col"), P("row", "col"))
    out_specs = (P("row", "col"), P("row", "col"))
    return jax.shard_map(body, mesh=mesh, in_specs=in_specs, out_specs=out_specs, check_vma=False)
```

time: 175 us -> 163 us (0.931)
  waiting for transfers between devices: 10.8 us -> 0.02 us
  Pallas kernels: 131 us -> 135 us
  matrix products: 8.44 us -> 4.5 us
  local copies, waits for them, and re-layouts: 10.8 us -> 8.1 us
    all_gather x2 -> x0, waiting for transfers between devices: 10.1 us -> none  [the longest x1 10.1 us: body(): solved = lax.all_gather(solved_prev, 'row', axis=0, tiled=True)]
    pallas_call x1, Pallas kernels: 87.2 us -> 91.2 us  [updated(): pl.pallas_call(functools.partial(update_kernel, rows_n, cols_n), out_shap...]
    dot_general x2 -> x1, matrix products: 5.27 us -> 1.32 us  [body(): lax.dot_general(update, lax.dynamic_slice_in_dim(inverse, col_place * w,...]
    unnamed x10 -> x14, local copies, waits for them, and re-layouts: 8.05 us -> 8.1 us
  transfers between devices with their start and end apart: 3 -> 1, of which waited for: 1 -> 0; matrix products, arithmetic and copies ran while one was open for 1% -> 1% of each run, Pallas kernels for 75% -> 27%
where the time goes in v5:
time: 163 us; the launch traced here: 162 us
  Pallas kernels  135 us (83%)
  between operations  14.1 us (9%)
  local copies, waits for them, and re-layouts  8.1 us (5%)
  matrix products  4.5 us (3%)
    pallas_call x1, Pallas kernels, updated(): pl.pallas_call(functools.partial(update_kernel, rows_n, cols_n), out_shap...  91.2 us
    pallas_call x1, Pallas kernels, invert(): pl.pallas_call(inverse_kernel, out_shape=jax.ShapeDtypeStruct((size, size...  43.9 us
    unnamed x14, local copies, waits for them, and re-layouts  8.1 us
  transfers between devices with their start and end apart: 1, of which 0 were waited for; matrix products, arithmetic and copies ran while one was open for 1% of the time, Pallas kernels for 27%

profile of v5, /device:TPU:0, one launch (start us, length us, event | category | flops | bytes accessed | tf_op | source)
XLA Modules:
  0.0 161.8 jit_solution(12337644104507974216)
XLA Ops:
  7.2 0.0 all-gather.2.cloned.1.call-start
  7.2 0.0 copy-start.1
  7.2 1.0 copy-done.1
  8.3 0.0 copy-start.2
  8.3 1.0 copy-done.2
  9.3 0.0 copy-start.3
  9.3 0.9 copy-done.3
  10.2 0.0 copy-start.4
  10.2 0.9 copy-done.4
  11.2 91.2 %shard_map.59 = (f32[4,1024,256]{2,1,0:T(8,128)}, f32[256,1024]{1,0:T(8,128)}, f32[128,512]{1,0:T(8,128)}) custom-call(bf16[256,1024]{1,0:T(8,128)(2,1)S(1)} %copy-done.1, f32[256,256]{1,0:T(8,128)S(1)} %copy-done.3, bf16[512,512]{1,0:T(8,128)(2,1)S(1)} %copy-done.2, f32[128,512]{1,0:T(8,128)S(1)} %copy-done.4), custom_call_target="tpu_custom_call" | custom-call | flops 536870912 | bytes 201326592 | tf_op jit(solution)/shard_map/pallas_call | solution.py:394
  102.4 0.0 all-gather.2.cloned.1.call-update
  102.4 0.0 copy-start.5
  102.4 2.2 %copy-done.5 = f32[4,1024,256]{2,1,0:T(8,128)S(1)} copy-done((f32[4,1024,256]{2,1,0:T(8,128)S(1)}, f32[4,1024,256]{2,1,0:T(8,128)}, u32[]{:S(2)}) %copy-start.5) | copy-done | bytes 4194328
  104.6 0.0 copy-start.6
  104.6 43.9 %shard_map.60 = f32[1024,1024]{1,0:T(8,128)S(1)} custom-call(f32[4,1024,256]{2,1,0:T(8,128)S(1)} %copy-done.5), custom_call_target="tpu_custom_call" | custom-call | flops 4294967296 | bytes 201326592 | tf_op jit(solution)/shard_map/pallas_call | solution.py:120
  148.5 0.0 copy-start
  148.5 1.9 %copy-done = f32[1024,1024]{1,0:T(8,128)} copy-done((f32[1024,1024]{1,0:T(8,128)}, f32[1024,1024]{1,0:T(8,128)S(1)}, u32[]{:S(2)}) %copy-start) | copy-done | bytes 4194328
  150.5 0.0 copy-done.6
  150.5 1.3 fusion
  151.8 0.0 all-gather.2.cloned.1.call-done
  151.8 3.2 %fusion.2 = f32[128,512]{1,0:T(8,128)} fusion(f32[1024,512]{1,0:T(8,128)} %all-gather.2.cloned.1.call-done, f32[1024,1024]{1,0:T(8,128)} %copy-done, s32[]{:T(128)S(6)} %select_n.7), kind=kOutput, calls=%fused_computation.2 | convolution fusion | flops 402653184 | bytes 2883588 | tf_op jit(solution)/shard_map/dot_general | solution.py:434
Async XLA Ops:
  7.2 144.6 %all-gather.2.cloned.1.call-start = ((), (), s32[]{:S(2)}) async-start(), calls=%async_computation | async-start | bytes 2359296 | tf_op jit(solution)/shard_map/all_gather | solution.py:426
  7.2 1.0 copy-start.1
  8.3 1.0 copy-start.2
  9.3 0.9 copy-start.3
  10.2 0.9 copy-start.4
  102.4 2.2 %copy-start.5 = (f32[4,1024,256]{2,1,0:T(8,128)S(1)}, f32[4,1024,256]{2,1,0:T(8,128)}, u32[]{:S(2)}) copy-start(f32[4,1024,256]{2,1,0:T(8,128)} %get-tuple-element.6.d_ref) | copy-start | bytes 12582916
  104.6 45.9 %copy-start.6 = (f32[256,1024]{1,0:T(8,128)S(1)}, f32[256,1024]{1,0:T(8,128)}, u32[]{:S(2)}) copy-start(f32[256,1024]{1,0:T(8,128)} %get-tuple-element.5) | copy-start | bytes 3145732
  148.5 1.9 %copy-start = (f32[1024,1024]{1,0:T(8,128)}, f32[1024,1024]{1,0:T(8,128)S(1)}, u32[]{:S(2)}) copy-start(f32[1024,1024]{1,0:T(8,128)S(1)} %shard_map.60) | copy-start | bytes 12582916
Sparse Core Ops, SparseCore 0:
  102.5 28.8 all-gather.1

commit v6 on v5

--- a/solution.py
+++ b/solution.py
@@ -9,6 +9,7 @@
 
 STRIP = 8
 TILE = 128
+TALL = 256
 
 
 def halves(value):
@@ -79,16 +80,34 @@
     return jnp.concatenate(done, axis=0)
 
 
+def travels(q, j, count):
+    gap = (j + count - q) % count
+    return (2 * gap < count) | ((2 * gap == count) & (2 * q < count))
+
+
 def inverse_kernel(d_ref, o_ref, w_ref):
     pieces, size, width = d_ref.shape
     count = size // TILE
     for q in range(pieces):
-        w_ref[:, q * width : (q + 1) * width] = d_ref[q]
+        rows = slice(q * width, (q + 1) * width)
+        for j in range(q, pieces):
+            block = d_ref[j, rows, :] if travels(q, j, pieces) else d_ref[q, j * width : (j + 1) * width, :].T
+            w_ref[rows, j * width : (j + 1) * width] = block
     lane = lax.broadcasted_iota(jnp.int32, (TILE, size), 1)
     eye = (
         lax.broadcasted_iota(jnp.int32, (TILE, TILE), 0)
         == lax.broadcasted_iota(jnp.int32, (TILE, TILE), 1)
     ).astype(jnp.float32)
+    across, down = [], []
+    for i in range(count):
+        tile = slice(i * TILE, (i + 1) * TILE)
+        only = jnp.where(eye > 0, w_ref[tile, tile], 0.0)
+        across.append(lax.rsqrt(jnp.sum(only, axis=0, keepdims=True)))
+        down.append(lax.rsqrt(jnp.sum(only, axis=1, keepdims=True)))
+    scale = jnp.concatenate(across, axis=1)
+    for i in range(count):
+        tile = slice(i * TILE, (i + 1) * TILE)
+        w_ref[tile, i * TILE :] = w_ref[tile, i * TILE :] * down[i] * scale[:, i * TILE :]
 
     def step(k, carry):
         at = pl.multiple_of(k * TILE, TILE)
@@ -96,20 +115,22 @@
         small = invert_tile(w_ref[here, here])
         w_ref[here, here] = eye
         z = dot3(small, w_ref[here, :])
-        o_ref[here, :] = jnp.where(lane < at + TILE, z, 0.0)
+        o_ref[here, :] = jnp.where(lane < at + TILE, z * scale, 0.0)
         w_ref[here, :] = z
         zh, zl = halves(z)
         right = jnp.concatenate([zh, zl, zh], axis=0)
 
         def trail(i, c):
-            mine = pl.ds(pl.multiple_of(i * TILE, TILE), TILE)
-            yh, yl = halves(w_ref[here, mine].T)
+            start = pl.multiple_of(i * TALL, TALL)
+            mine = pl.ds(start, TALL)
+            later = start + lax.broadcasted_iota(jnp.int32, (TALL, TILE), 0) >= at + TILE
+            yh, yl = halves(jnp.where(later, w_ref[here, mine].T, 0.0))
             left = jnp.concatenate([yh, yh, yl], axis=1)
-            w_ref[mine, here] = jnp.zeros((TILE, TILE), jnp.float32)
+            w_ref[mine, here] = jnp.where(later, 0.0, w_ref[mine, here])
             w_ref[mine, :] -= jnp.dot(left, right, preferred_element_type=jnp.float32)
             return c
 
-        lax.fori_loop(k + 1, count, trail, 0)
+        lax.fori_loop((k + 1) // (TALL // TILE), size // TALL, trail, 0)
         return carry
 
     lax.fori_loop(0, count, step, 0)
@@ -156,9 +177,15 @@
 
 
 class RowGather:
-    def __init__(self, at, own, block, send, recv, side_send, side_recv):
-        self.at, self.own, self.block = at, own, block
+    def __init__(self, at, own, block, send, recv, side_send, side_recv, wanted=None):
+        self.at, self.own, self.block, self.wanted = at, own, block, wanted
         self.send, self.recv, self.side_send, self.side_recv = send, recv, side_send, side_recv
+
+    def when(self, s, act):
+        if self.wanted is None:
+            act()
+        else:
+            pl.when(self.wanted(self.at.origin(s)))(act)
 
     def far(self, s):
         at = self.at
@@ -181,14 +208,20 @@
         return copy(block, block, self.side_send(s), self.side_recv(s), at.sibling)
 
     def start(self):
-        for s in range(1, self.at.chips):
-            self.far(s).start()
-        self.near(0).start()
+        def act():
+            for s in range(1, self.at.chips):
+                self.far(s).start()
+            self.near(0).start()
+
+        self.when(0, act)
 
     def relay(self, s):
-        if s > 0:
+        def act():
             self.far_in(s).wait_recv()
             self.near(s).start()
+
+        if s > 0:
+            self.when(s, act)
 
     def relay_all(self):
         for s in range(1, self.at.chips):
@@ -196,13 +229,16 @@
 
     def arrive(self):
         for s in range(self.at.chips):
-            self.near_in(s).wait_recv()
+            self.when(s, lambda s=s: self.near_in(s).wait_recv())
 
     def finish(self):
+        def act():
+            for s in range(1, self.at.chips):
+                self.far(s).wait_send()
+
+        self.when(0, act)
         for s in range(self.at.chips):
-            if s > 0:
-                self.far(s).wait_send()
-            self.near(s).wait_send()
+            self.when(s, lambda s=s: self.near(s).wait_send())
 
 
 class ColGather:
@@ -296,7 +332,8 @@
     def piece(q):
         return RowGather(
             at, d_ref.at[q, span(r, b)], lambda i: d_ref.at[q, span(i, b)],
-            *[lambda s, ref=ref: ref.at[q, s] for ref in (d_send, d_recv, ds_send, ds_recv)]
+            *[lambda s, ref=ref: ref.at[q, s] for ref in (d_send, d_recv, ds_send, ds_recv)],
+            wanted=lambda i: travels(i, q, cols_n),
         )
 
     def pieces(t, act):

time: 163 us -> 154 us (0.945)
  Pallas kernels: 135 us -> 126 us
    pallas_call x1, Pallas kernels: 91.2 us -> 83.9 us  [updated(): pl.pallas_call(functools.partial(update_kernel, rows_n, cols_n), out_shap...]
    pallas_call x1, Pallas kernels: 43.9 us -> 41.7 us  [invert(): pl.pallas_call(inverse_kernel, out_shape=jax.ShapeDtypeStruct((size, size...]
where the time goes in v6:
time: 154 us; the launch traced here: 152 us
  Pallas kernels  126 us (82%)
  between operations  14.1 us (9%)
  local copies, waits for them, and re-layouts  8.1 us (5%)
  matrix products  4.5 us (3%)
    pallas_call x1, Pallas kernels, updated(): pl.pallas_call(functools.partial(update_kernel, rows_n, cols_n), out_shap...  83.9 us
    pallas_call x1, Pallas kernels, invert(): pl.pallas_call(inverse_kernel, out_shape=jax.ShapeDtypeStruct((size, size...  41.7 us
    unnamed x14, local copies, waits for them, and re-layouts  8.1 us
    dot_general x1, matrix products, body(): jnp.dot(lax.dynamic_slice_in_dim(inverse, row_place * b, b, 0), reduced,...  3.18 us
  transfers between devices with their start and end apart: 1, of which 0 were waited for; matrix products, arithmetic and copies ran while one was open for 1% of the time, Pallas kernels for 27%

profile of v6, /device:TPU:0, one launch (start us, length us, event | category | flops | bytes accessed | tf_op | source)
XLA Modules:
  0.0 152.3 jit_solution(13737807186824351740)
XLA Ops:
  7.2 0.0 all-gather.2.cloned.1.call-start
  7.2 0.0 copy-start.1
  7.2 1.0 copy-done.1
  8.3 0.0 copy-start.2
  8.3 1.0 copy-done.2
  9.3 0.0 copy-start.3
  9.3 0.9 copy-done.3
  10.2 0.0 copy-start.4
  10.2 0.9 copy-done.4
  11.2 83.9 %shard_map.59 = (f32[4,1024,256]{2,1,0:T(8,128)}, f32[256,1024]{1,0:T(8,128)}, f32[128,512]{1,0:T(8,128)}) custom-call(bf16[256,1024]{1,0:T(8,128)(2,1)S(1)} %copy-done.1, f32[256,256]{1,0:T(8,128)S(1)} %copy-done.3, bf16[512,512]{1,0:T(8,128)(2,1)S(1)} %copy-done.2, f32[128,512]{1,0:T(8,128)S(1)} %copy-done.4), custom_call_target="tpu_custom_call" | custom-call | flops 536870912 | bytes 201326592 | tf_op jit(solution)/shard_map/pallas_call | solution.py:431
  95.1 0.0 all-gather.2.cloned.1.call-update
  95.1 0.0 copy-start.5
  95.1 2.2 %copy-done.5 = f32[4,1024,256]{2,1,0:T(8,128)S(1)} copy-done((f32[4,1024,256]{2,1,0:T(8,128)S(1)}, f32[4,1024,256]{2,1,0:T(8,128)}, u32[]{:S(2)}) %copy-start.5) | copy-done | bytes 4194328
  97.3 0.0 copy-start.6
  97.3 41.7 %shard_map.60 = f32[1024,1024]{1,0:T(8,128)S(1)} custom-call(f32[4,1024,256]{2,1,0:T(8,128)S(1)} %copy-done.5), custom_call_target="tpu_custom_call" | custom-call | flops 4294967296 | bytes 201326592 | tf_op jit(solution)/shard_map/pallas_call | solution.py:141
  139.0 0.0 copy-start
  139.0 1.9 %copy-done = f32[1024,1024]{1,0:T(8,128)} copy-done((f32[1024,1024]{1,0:T(8,128)}, f32[1024,1024]{1,0:T(8,128)S(1)}, u32[]{:S(2)}) %copy-start) | copy-done | bytes 4194328
  140.9 0.0 copy-done.6
  140.9 1.3 fusion
  142.3 0.0 all-gather.2.cloned.1.call-done
  142.3 3.2 %fusion.2 = f32[128,512]{1,0:T(8,128)} fusion(f32[1024,512]{1,0:T(8,128)} %all-gather.2.cloned.1.call-done, f32[1024,1024]{1,0:T(8,128)} %copy-done, s32[]{:T(128)S(6)} %select_n.7), kind=kOutput, calls=%fused_computation.2 | convolution fusion | flops 402653184 | bytes 2883588 | tf_op jit(solution)/shard_map/dot_general | solution.py:471
Async XLA Ops:
  7.2 135.1 %all-gather.2.cloned.1.call-start = ((), (), s32[]{:S(2)}) async-start(), calls=%async_computation | async-start | bytes 2359296 | tf_op jit(solution)/shard_map/all_gather | solution.py:463
  7.2 1.0 copy-start.1
  8.3 1.0 copy-start.2
  9.3 0.9 copy-start.3
  10.2 0.9 copy-start.4
  95.1 2.2 %copy-start.5 = (f32[4,1024,256]{2,1,0:T(8,128)S(1)}, f32[4,1024,256]{2,1,0:T(8,128)}, u32[]{:S(2)}) copy-start(f32[4,1024,256]{2,1,0:T(8,128)} %get-tuple-element.6.d_ref) | copy-start | bytes 12582916
  97.3 43.7 %copy-start.6 = (f32[256,1024]{1,0:T(8,128)S(1)}, f32[256,1024]{1,0:T(8,128)}, u32[]{:S(2)}) copy-start(f32[256,1024]{1,0:T(8,128)} %get-tuple-element.5) | copy-start | bytes 3145732
  139.0 1.9 %copy-start = (f32[1024,1024]{1,0:T(8,128)}, f32[1024,1024]{1,0:T(8,128)S(1)}, u32[]{:S(2)}) copy-start(f32[1024,1024]{1,0:T(8,128)S(1)} %shard_map.60) | copy-start | bytes 12582916
Sparse Core Ops, SparseCore 0:
  95.2 29.6 all-gather.1

commit v7 on v6

--- a/solution.py
+++ b/solution.py
@@ -357,7 +357,10 @@
         top_out[q] = product(left_ref[:b], q)
         pl.when(q != c)(lambda: to_owner(q, top_out, top_in, *top_sems).start())
 
+    mine[c] = left_ref[:b]
+    others = ColGather(at, lambda q: mine.at[q], m_send, m_recv)
     first.start()
+    others.start()
     chosen[span(r, b), :] = left_ref[:b]
     for s in range(chips):
         first.relay(s)
@@ -365,13 +368,12 @@
             sent(max(s - 1, 0))
     second.start()
     sent(chips - 1)
-    mine[c] = left_ref[:b]
+    others.take(1)
     solved[span(r, deep), :] = solved_ref[...]
     for s in range(chips):
         low_out[at.origin(s)] = product(left_ref[b:], at.origin(s))
 
     across = ColGather(at, lambda q: d_ref.at[q, span(r, b)], z_send, z_recv)
-    others = ColGather(at, lambda q: mine.at[q], m_send, m_recv)
     lows = ColGather(at, lambda q: low_all.at[q], y_send, y_recv)
     d_ref[c, span(r, b), :] = total(gram_ref[:b], top_out, top_in, top_sems)
     across.start()
@@ -380,13 +382,12 @@
         to_owner((c + u) % cols_n, low_out, low_in, *low_sems).start()
     for t in range(1, cols_n):
         across.take(t, lambda q: piece(q).start())
-        if t == 1:
-            others.start()
+        if t > 1:
+            others.take(t)
         pieces(t - 1, lambda part: part.relay_all())
     low_all[c] = total(gram_ref[b:], low_out, low_in, low_sems)
     lows.start()
     for t in range(1, cols_n):
-        others.take(t)
         second.relay(t)
         lows.take(t)
     pieces(cols_n - 1, lambda part: part.relay_all())

time: 154 us -> 149 us (0.968); the launches traced: 152 us -> 149 us
  Pallas kernels: 126 us -> 122 us
    pallas_call x1, Pallas kernels: 83.9 us -> 80.7 us  [updated(): pl.pallas_call(functools.partial(update_kernel, rows_n, cols_n), out_shap...]
  transfers between devices with their start and end apart: 1 -> 1, of which waited for: 0 -> 0; matrix products, arithmetic and copies ran while one was open for 1% -> 1% of each run, Pallas kernels for 27% -> 28%
where the time goes in v7:
time: 149 us
  Pallas kernels  122 us (82%)
  between operations  14.1 us (9%)
  local copies, waits for them, and re-layouts  8.1 us (5%)
  matrix products  4.5 us (3%)
    pallas_call x1, Pallas kernels, updated(): pl.pallas_call(functools.partial(update_kernel, rows_n, cols_n), out_shap...  80.7 us
    pallas_call x1, Pallas kernels, invert(): pl.pallas_call(inverse_kernel, out_shape=jax.ShapeDtypeStruct((size, size...  41.7 us
    unnamed x14, local copies, waits for them, and re-layouts  8.1 us
    dot_general x1, matrix products, body(): jnp.dot(lax.dynamic_slice_in_dim(inverse, row_place * b, b, 0), reduced,...  3.18 us
  transfers between devices with their start and end apart: 1, of which 0 were waited for; matrix products, arithmetic and copies ran while one was open for 1% of the time, Pallas kernels for 28%

profile of v7, /device:TPU:0, one launch (start us, length us, event | category | flops | bytes accessed | tf_op | source)
XLA Modules:
  0.0 149.1 jit_solution(2626545310989471418)
XLA Ops:
  7.2 0.0 all-gather.2.cloned.1.call-start
  7.2 0.0 copy-start.1
  7.2 1.0 copy-done.1
  8.3 0.0 copy-start.2
  8.3 1.0 copy-done.2
  9.3 0.0 copy-start.3
  9.3 0.9 copy-done.3
  10.2 0.0 copy-start.4
  10.2 0.9 copy-done.4
  11.2 80.7 %shard_map.59 = (f32[4,1024,256]{2,1,0:T(8,128)}, f32[256,1024]{1,0:T(8,128)}, f32[128,512]{1,0:T(8,128)}) custom-call(bf16[256,1024]{1,0:T(8,128)(2,1)S(1)} %copy-done.1, f32[256,256]{1,0:T(8,128)S(1)} %copy-done.3, bf16[512,512]{1,0:T(8,128)(2,1)S(1)} %copy-done.2, f32[128,512]{1,0:T(8,128)S(1)} %copy-done.4), custom_call_target="tpu_custom_call" | custom-call | flops 536870912 | bytes 201326592 | tf_op jit(solution)/shard_map/pallas_call | solution.py:432
  91.9 0.0 all-gather.2.cloned.1.call-update
  91.9 0.0 copy-start.5
  92.0 2.2 %copy-done.5 = f32[4,1024,256]{2,1,0:T(8,128)S(1)} copy-done((f32[4,1024,256]{2,1,0:T(8,128)S(1)}, f32[4,1024,256]{2,1,0:T(8,128)}, u32[]{:S(2)}) %copy-start.5) | copy-done | bytes 4194328
  94.1 0.0 copy-start.6
  94.1 41.7 %shard_map.60 = f32[1024,1024]{1,0:T(8,128)S(1)} custom-call(f32[4,1024,256]{2,1,0:T(8,128)S(1)} %copy-done.5), custom_call_target="tpu_custom_call" | custom-call | flops 4294967296 | bytes 201326592 | tf_op jit(solution)/shard_map/pallas_call | solution.py:141
  135.8 0.0 copy-start
  135.9 1.9 %copy-done = f32[1024,1024]{1,0:T(8,128)} copy-done((f32[1024,1024]{1,0:T(8,128)}, f32[1024,1024]{1,0:T(8,128)S(1)}, u32[]{:S(2)}) %copy-start) | copy-done | bytes 4194328
  137.8 0.0 copy-done.6
  137.8 1.3 fusion
  139.1 0.0 all-gather.2.cloned.1.call-done
  139.1 3.2 %fusion.2 = f32[128,512]{1,0:T(8,128)} fusion(f32[1024,512]{1,0:T(8,128)} %all-gather.2.cloned.1.call-done, f32[1024,1024]{1,0:T(8,128)} %copy-done, s32[]{:T(128)S(6)} %select_n.7), kind=kOutput, calls=%fused_computation.2 | convolution fusion | flops 402653184 | bytes 2883588 | tf_op jit(solution)/shard_map/dot_general | solution.py:472
Async XLA Ops:
  7.2 132.0 %all-gather.2.cloned.1.call-start = ((), (), s32[]{:S(2)}) async-start(), calls=%async_computation | async-start | bytes 2359296 | tf_op jit(solution)/shard_map/all_gather | solution.py:464
  7.2 1.0 copy-start.1
  8.3 1.0 copy-start.2
  9.3 0.9 copy-start.3
  10.2 0.9 copy-start.4
  91.9 2.2 %copy-start.5 = (f32[4,1024,256]{2,1,0:T(8,128)S(1)}, f32[4,1024,256]{2,1,0:T(8,128)}, u32[]{:S(2)}) copy-start(f32[4,1024,256]{2,1,0:T(8,128)} %get-tuple-element.6.d_ref) | copy-start | bytes 12582916
  94.1 43.7 %copy-start.6 = (f32[256,1024]{1,0:T(8,128)S(1)}, f32[256,1024]{1,0:T(8,128)}, u32[]{:S(2)}) copy-start(f32[256,1024]{1,0:T(8,128)} %get-tuple-element.5) | copy-start | bytes 3145732
  135.8 1.9 %copy-start = (f32[1024,1024]{1,0:T(8,128)}, f32[1024,1024]{1,0:T(8,128)S(1)}, u32[]{:S(2)}) copy-start(f32[1024,1024]{1,0:T(8,128)S(1)} %shard_map.60) | copy-start | bytes 12582916
Sparse Core Ops, SparseCore 0:
  92.1 27.1 all-gather.1
